TPU v7x, 256 devices: a whole 4x4x8 slice. The times are simulated.
256 devices in a mesh: row: 16 (over z_lo, y, core), col: 16 (over z_hi, x).
Axes of the slice: x: 4, y: 4, z: 8 (z_hi: 4, z_lo: 2; z = z_hi * 2 + z_lo), core: 2. Of those that a mesh axis runs over, the one named last changes fastest.
Arguments:
- source_desc: bfloat16 [32768, 64], P('row', 'col'), may hold values from -9 to 9
- target_desc: bfloat16 [32768, 64], P('col'), may hold values from -9 to 9
- source_mass: bfloat16 [32768], P('row'), may hold values from 0.099609375 to 10
- target_mass: bfloat16 [32768], P('col'), may hold values from 0.099609375 to 10
Outputs:
- cross_source: float32 [32768], P('row')
- cross_target: float32 [32768], P('col')
- self_source: float32 [32768], P('row')
- self_target: float32 [32768], P('col')
All inputs are finite; a program needn't handle non-finite values.
Results may differ from a plain program's by a relative error of at most 0.0003.
Values may be sent and summed in bfloat16 or wider, within the bound.
A program may use at most 64 MiB of HBM per device.

v0:
```python
import math

import jax
import jax.numpy as jnp
from jax import lax
from jax.sharding import PartitionSpec as P

ITERS = 2


EPSILON = 0.25
REACH = 1.0
DAMPING = 1.0 / (1.0 + EPSILON / REACH)


def half_norms(points):
    wide = points.astype(jnp.float32)
    return 0.5 * jnp.sum(wide * wide, axis=1)


def tile_stats(
    left_desc, right_desc, left_norm, right_norm, left_weight, right_weight, want_rows, want_cols
):
    count = left_desc.shape[0]
    block = math.gcd(512, count)
    blocks = count // block
    width = left_desc.shape[1]
    right_count = right_desc.shape[0]
    inputs = (
        left_desc.reshape(blocks, block, width),
        left_norm.reshape(blocks, block),
        left_weight.reshape(blocks, block),
    )

    def advance(carry, pieces):
        piece_desc, piece_norm, piece_weight = pieces
        product = lax.dot_general(
            piece_desc, right_desc, (((1,), (1,)), ((), ())), preferred_element_type=jnp.float32
        )
        scaled = (piece_norm[:, None] + right_norm[None, :] - product) / EPSILON
        emitted = ()
        if want_rows:
            row_score = right_weight[None, :] - scaled
            row_top = jnp.max(row_score, axis=1)
            row_total = jnp.sum(jnp.exp(row_score - row_top[:, None]), axis=1)
            emitted = (row_top, row_total)
        if want_cols:
            col_top, col_total = carry
            col_score = piece_weight[:, None] - scaled
            fresh_top = jnp.maximum(col_top, jnp.max(col_score, axis=0))
            col_total = col_total * jnp.exp(col_top - fresh_top) + jnp.sum(
                jnp.exp(col_score - fresh_top[None, :]), axis=0
            )
            carry = (fresh_top, col_total)
        return (carry, emitted)

    if want_cols:
        start = (
            jnp.full((right_count,), -jnp.inf, jnp.float32),
            jnp.zeros((right_count,), jnp.float32),
        )
    else:
        start = ()
    carry, emitted = lax.scan(advance, start, inputs)
    rows_out = (emitted[0].reshape(count), emitted[1].reshape(count)) if want_rows else None
    cols_out = carry if want_cols else None
    return (rows_out, cols_out)


def reduce_col(maxima, totals):
    merged_top = lax.pmax(maxima, "col")
    merged_total = lax.psum(totals * jnp.exp(maxima - merged_top), "col")
    return merged_top + jnp.log(merged_total)


def reduce_row(maxima, totals):
    merged_top = lax.pmax(maxima, "row")
    merged_total = lax.psum(totals * jnp.exp(maxima - merged_top), "row")
    return merged_top + jnp.log(merged_total)


def body(source_desc, target_desc, source_mass, target_mass):
    row_devices = lax.axis_size("row")
    col_devices = lax.axis_size("col")
    row_index = lax.axis_index("row")
    col_index = lax.axis_index("col")
    tile_count = source_mass.shape[0]
    source_part = tile_count // col_devices
    target_part = target_desc.shape[0] // row_devices
    mass_piece = lax.dynamic_slice_in_dim(source_mass, col_index * source_part, source_part, 0)
    source_rows = lax.all_gather(source_desc, "col", axis=1, tiled=True)
    desc_piece = lax.dynamic_slice_in_dim(source_rows, col_index * source_part, source_part, 0)
    source_cols, source_col_mass = (
        lax.all_gather(desc_piece, "row", axis=0, tiled=True),
        lax.all_gather(mass_piece, "row", axis=0, tiled=True),
    )
    target_piece = lax.dynamic_slice_in_dim(target_desc, row_index * target_part, target_part, 0)
    target_mass_piece = lax.dynamic_slice_in_dim(
        target_mass, row_index * target_part, target_part, 0
    )
    target_rows, target_row_mass = (
        lax.all_gather(target_piece, "col", axis=0, tiled=True),
        lax.all_gather(target_mass_piece, "col", axis=0, tiled=True),
    )
    source_log = jnp.log(source_mass.astype(jnp.float32))
    source_col_log = jnp.log(source_col_mass.astype(jnp.float32))
    target_log = jnp.log(target_mass.astype(jnp.float32))
    target_row_log = jnp.log(target_row_mass.astype(jnp.float32))
    source_row_norm = half_norms(source_rows)
    source_col_norm = half_norms(source_cols)
    target_col_norm = half_norms(target_desc)
    target_row_norm = half_norms(target_rows)
    cross_source = jnp.zeros((tile_count,), jnp.float32)
    cross_target = jnp.zeros((target_desc.shape[0],), jnp.float32)
    self_source = jnp.zeros((tile_count,), jnp.float32)
    self_target = jnp.zeros((target_desc.shape[0],), jnp.float32)
    source_view = jnp.zeros((source_cols.shape[0],), jnp.float32)
    target_view = jnp.zeros((target_rows.shape[0],), jnp.float32)
    for iteration in range(ITERS):
        mirror_work = iteration + 1 < ITERS
        cross_rows, cross_cols = tile_stats(
            source_rows,
            target_desc,
            source_row_norm,
            target_col_norm,
            source_log + cross_source / EPSILON,
            target_log + cross_target / EPSILON,
            True,
            True,
        )
        source_self_rows, source_self_cols = tile_stats(
            source_rows,
            source_cols,
            source_row_norm,
            source_col_norm,
            source_log + self_source / EPSILON,
            source_col_log + source_view / EPSILON,
            True,
            mirror_work,
        )
        target_self_rows, target_self_cols = tile_stats(
            target_rows,
            target_desc,
            target_row_norm,
            target_col_norm,
            target_row_log + target_view / EPSILON,
            target_log + self_target / EPSILON,
            mirror_work,
            True,
        )
        col_maxima = [cross_rows[0], source_self_rows[0]]
        col_totals = [cross_rows[1], source_self_rows[1]]
        row_maxima = [cross_cols[0], target_self_cols[0]]
        row_totals = [cross_cols[1], target_self_cols[1]]
        if mirror_work:
            col_maxima.append(target_self_rows[0])
            col_totals.append(target_self_rows[1])
            row_maxima.append(source_self_cols[0])
            row_totals.append(source_self_cols[1])
        col_logs = reduce_col(jnp.concatenate(col_maxima), jnp.concatenate(col_totals))
        row_logs = reduce_row(jnp.concatenate(row_maxima), jnp.concatenate(row_totals))
        target_count = target_desc.shape[0]
        cross_source = 0.5 * cross_source + 0.5 * DAMPING * (-EPSILON * col_logs[:tile_count])
        self_source = 0.5 * self_source + 0.5 * DAMPING * (
            -EPSILON * col_logs[tile_count : 2 * tile_count]
        )
        cross_target = 0.5 * cross_target + 0.5 * DAMPING * (-EPSILON * row_logs[:target_count])
        self_target = 0.5 * self_target + 0.5 * DAMPING * (
            -EPSILON * row_logs[target_count : 2 * target_count]
        )
        if mirror_work:
            target_view = 0.5 * target_view + 0.5 * DAMPING * (
                -EPSILON * col_logs[2 * tile_count :]
            )
            source_view = 0.5 * source_view + 0.5 * DAMPING * (
                -EPSILON * row_logs[2 * target_count :]
            )
    return (cross_source, cross_target, self_source, self_target)


def solution(mesh):
    return jax.shard_map(
        body,
        mesh=mesh,
        in_specs=(P("row", "col"), P("col", None), P("row"), P("col")),
        out_specs=(P("row"), P("col"), P("row"), P("col")),
        check_vma=False,
    )
```

profile of v0, /device:TPU:32, one launch (start us, length us, event | category | flops | bytes accessed | tf_op | source)
XLA Modules:
  0.0 824.4 jit_solution(18188859646712844108)
XLA Ops:
  0.6 47.2 %all-gather = bf16[16,4,2048]{2,1,0:T(4,128)(2,1)S(1)} all-gather(bf16[1,4,2048]{2,1,0:T(4,128)(2,1)} %bitcast.208), channel_id=1, replica_groups=mesh['row'=16,'col'=16] {'col'}, dimensions={0}, use_global_device_ids=true | all-gather | bytes 278528 | tf_op jit(solution)/shard_map/all_gather | solution.py:91
  47.9 20.2 %all_gather.16 = bf16[2048,64]{0,1:T(8,128)(2,1)S(1)} all-gather(bf16[128,64]{0,1:T(8,128)(2,1)S(1)} %dynamic-slice_bitcast_fusion), channel_id=1, replica_groups=mesh['row'=16,'col'=16] {'row'}, dimensions={0}, use_global_device_ids=true | all-gather | bytes 278528 | tf_op jit(solution)/shard_map/all_gather | solution.py:94
  68.5 0.8 dynamic-slice_bitcast_fusion.2
  69.3 16.1 %all-gather.1 = bf16[16,1,128]{2,1,0:T(2,128)(2,1)S(1)} all-gather(bf16[1,1,128]{2,1,0:T(2,128)(2,1)S(1)} %dynamic-slice_bitcast_fusion.2), channel_id=1, replica_groups=mesh['row'=16,'col'=16] {'row'}, dimensions={0}, use_global_device_ids=true | all-gather | bytes 4352 | tf_op jit(solution)/shard_map/all_gather | solution.py:95
  86.6 26.9 %while.95 = (s32[]{:T(128)}, f32[2048]{0:T(1024)S(1)}, f32[2048]{0:T(1024)S(1)}, f32[4,512]{1,0:T(4,128)S(1)}, f32[4,512]{1,0:T(4,128)S(1)}, /*index=5*/f32[4,51...) while((s32[]{:T(128)}, f32[2048]{0:T(1024)S(1)}, ...), condition=%wide.region_14.15_spmd.clone, body=%wide.region_9.14_spmd.clone.sunk | while | flops 147858432 | bytes 9203864 | solution.py:64
  86.6 3.2 subtract_reduce_fusion.13
  89.8 3.4 exponential_reduce_fusion.18
  93.3 3.2 subtract_reduce_fusion.13
  96.5 3.4 exponential_reduce_fusion.18
  100.1 3.2 subtract_reduce_fusion.13
  103.3 3.4 exponential_reduce_fusion.18
  106.8 3.2 subtract_reduce_fusion.13
  110.0 3.4 exponential_reduce_fusion.18
  113.7 26.7 %while.94 = (s32[]{:T(128)}, f32[2048]{0:T(1024)S(1)}, f32[2048]{0:T(1024)S(1)}, f32[4,512]{1,0:T(4,128)S(1)}, f32[4,512]{1,0:T(4,128)S(1)}, /*index=5*/f32[4,51...) while((s32[]{:T(128)}, f32[2048]{0:T(1024)S(1)}, ...), condition=%wide.region_7.8_spmd.clone, body=%wide.region_2.7_spmd.clone.sunk | while | flops 147858432 | bytes 8941720 | solution.py:64
  113.7 3.1 subtract_reduce_fusion.12
  116.9 3.4 exponential_reduce_fusion.17
  120.4 3.1 subtract_reduce_fusion.12
  123.6 3.4 exponential_reduce_fusion.17
  127.1 3.1 subtract_reduce_fusion.12
  130.2 3.4 exponential_reduce_fusion.17
  133.8 3.1 subtract_reduce_fusion.12
  136.9 3.4 exponential_reduce_fusion.17
  140.5 39.3 %all_gather.19 = bf16[2048,64]{0,1:T(8,128)(2,1)S(1)} all-gather(bf16[128,64]{0,1:T(8,128)(2,1)S(1)} %constant_dynamic-slice_fusion.11), channel_id=1, replica_groups=mesh['row'=16,'col'=16] {'col'}, dimensions={0}, use_global_device_ids=true | all-gather | bytes 278528 | tf_op jit(solution)/shard_map/all_gather | solution.py:102
  180.3 39.8 %all-gather.2 = bf16[16,1,128]{2,1,0:T(2,128)(2,1)S(1)} all-gather(bf16[1,1,128]{2,1,0:T(2,128)(2,1)S(1)} %dynamic-slice_bitcast_fusion.1), channel_id=1, replica_groups=mesh['row'=16,'col'=16] {'col'}, dimensions={0}, use_global_device_ids=true | all-gather | bytes 4352 | tf_op jit(solution)/shard_map/all_gather | solution.py:103
  220.2 26.7 %while.96 = (s32[]{:T(128)}, f32[2048]{0:T(1024)S(1)}, f32[2048]{0:T(1024)S(1)}, f32[4,512]{1,0:T(4,128)S(1)}, f32[4,512]{1,0:T(4,128)S(1)}, /*index=5*/f32[4,51...) while((s32[]{:T(128)}, f32[2048]{0:T(1024)S(1)}, ...), condition=%wide.region_21.22_spmd.clone, body=%wide.region_16.21_spmd.clone.sunk | while | flops 147858432 | bytes 8941720 | solution.py:64
  220.2 3.1 subtract_reduce_fusion.14
  223.3 3.4 exponential_reduce_fusion.19
  226.9 3.1 subtract_reduce_fusion.14
  230.0 3.4 exponential_reduce_fusion.19
  233.6 3.1 subtract_reduce_fusion.14
  236.7 3.4 exponential_reduce_fusion.19
  240.2 3.1 subtract_reduce_fusion.14
  243.4 3.4 exponential_reduce_fusion.19
  246.9 76.7 %pmax.28 = f32[6144]{0:T(1024)S(1)} all-reduce(f32[6144]{0:T(1024)S(1)} %constant_dynamic-update-slice_fusion.8), channel_id=1, replica_groups=mesh['row'=16,'col'=16] {'col'}, use_global_device_ids=true, to_apply=%region_22.23 | all-reduce | flops 6144 | bytes 49152 | tf_op jit(solution)/shard_map/pmax | solution.py:71
  323.7 76.7 %psum.28 = f32[6144]{0:T(1024)S(1)} all-reduce(f32[6144]{0:T(1024)S(1)} %maximum_multiply_fusion), channel_id=1, replica_groups=mesh['row'=16,'col'=16] {'col'}, use_global_device_ids=true, to_apply=%region_23.24 | all-reduce | flops 6144 | bytes 49152 | tf_op jit(solution)/shard_map/psum | solution.py:72
  400.5 22.8 %while.98 = (s32[]{:T(128)}, f32[2048]{0:T(1024)S(1)}, f32[2048]{0:T(1024)S(1)}, f32[4,512]{1,0:T(4,128)S(1)}, f32[4,512]{1,0:T(4,128)S(1)}, /*index=5*/f32[2048...) while((s32[]{:T(128)}, f32[2048]{0:T(1024)S(1)}, ...), condition=%wide.region_41.42_spmd.clone, body=%wide.region_38.0_spmd.clone.sunk | while | flops 141568000 | bytes 8908920 | solution.py:64
  400.5 2.9 fusion.62
  403.4 2.8 exponential_reduce_fusion.21
  406.2 2.8 fusion.62
  409.1 2.8 exponential_reduce_fusion.21
  411.9 2.8 fusion.62
  414.8 2.8 exponential_reduce_fusion.21
  417.6 2.8 fusion.62
  420.5 2.8 exponential_reduce_fusion.21
  423.3 53.0 %pmax.29 = f32[6144]{0:T(1024)S(1)} all-reduce(f32[6144]{0:T(1024)S(1)} %constant_dynamic-update-slice_fusion.9), channel_id=1, replica_groups=mesh['row'=16,'col'=16] {'row'}, use_global_device_ids=true, to_apply=%region_24.25 | all-reduce | flops 6144 | bytes 49152 | tf_op jit(solution)/shard_map/pmax | solution.py:77
  476.3 53.1 %psum.29 = f32[6144]{0:T(1024)S(1)} all-reduce(f32[6144]{0:T(1024)S(1)} %maximum_multiply_fusion.1), channel_id=1, replica_groups=mesh['row'=16,'col'=16] {'row'}, use_global_device_ids=true, to_apply=%region_25.26 | all-reduce | flops 6144 | bytes 49152 | tf_op jit(solution)/shard_map/psum | solution.py:78
  529.5 26.7 %while.97 = (s32[]{:T(128)}, f32[2048]{0:T(1024)S(1)}, f32[2048]{0:T(1024)S(1)}, f32[4,512]{1,0:T(4,128)S(1)}, f32[4,512]{1,0:T(4,128)S(1)}, /*index=5*/f32[4,51...) while((s32[]{:T(128)}, f32[2048]{0:T(1024)S(1)}, ...), condition=%wide.region_31.32_spmd.clone, body=%wide.region_26.31_spmd.clone.sunk | while | flops 147858432 | bytes 8941720 | solution.py:64
  529.5 3.1 subtract_reduce_fusion.15
  532.7 3.4 exponential_reduce_fusion.20
  536.2 3.1 subtract_reduce_fusion.15
  539.4 3.4 exponential_reduce_fusion.20
  542.9 3.1 subtract_reduce_fusion.15
  546.1 3.4 exponential_reduce_fusion.20
  549.6 3.1 subtract_reduce_fusion.15
  552.7 3.4 exponential_reduce_fusion.20
  556.3 52.9 %pmax.31 = f32[4096]{0:T(1024)S(1)} all-reduce(f32[4096]{0:T(1024)S(1)} %constant_dynamic-update-slice_fusion.3), channel_id=1, replica_groups=mesh['row'=16,'col'=16] {'row'}, use_global_device_ids=true, to_apply=%region_42.43 | all-reduce | flops 4096 | bytes 32768 | tf_op jit(solution)/shard_map/pmax | solution.py:77
  609.2 52.9 %psum.31 = f32[4096]{0:T(1024)S(1)} all-reduce(f32[4096]{0:T(1024)S(1)} %maximum_multiply_fusion.3), channel_id=1, replica_groups=mesh['row'=16,'col'=16] {'row'}, use_global_device_ids=true, to_apply=%region_43.44 | all-reduce | flops 4096 | bytes 32768 | tf_op jit(solution)/shard_map/psum | solution.py:78
  662.8 7.4 while.93
  662.8 1.0 fusion.52
  664.7 1.0 fusion.52
  666.5 1.0 fusion.52
  668.4 1.0 fusion.52
  670.3 76.7 %pmax.30 = f32[4096]{0:T(1024)S(1)} all-reduce(f32[4096]{0:T(1024)S(1)} %constant_dynamic-update-slice_fusion.2), channel_id=1, replica_groups=mesh['row'=16,'col'=16] {'col'}, use_global_device_ids=true, to_apply=%region_36.37 | all-reduce | flops 4096 | bytes 32768 | tf_op jit(solution)/shard_map/pmax | solution.py:71
  747.0 76.7 %psum.30 = f32[4096]{0:T(1024)S(1)} all-reduce(f32[4096]{0:T(1024)S(1)} %maximum_multiply_fusion.2), channel_id=1, replica_groups=mesh['row'=16,'col'=16] {'col'}, use_global_device_ids=true, to_apply=%region_37.38 | all-reduce | flops 4096 | bytes 32768 | tf_op jit(solution)/shard_map/psum | solution.py:72
  (211 shorter events, 9.0 us)
Async XLA Ops:
  86.5 27.0 %copy-start = (bf16[2048,64]{0,1:T(8,128)(2,1)S(1)}, bf16[2048,64]{0,1:T(8,128)(2,1)}, u32[]{:S(2)}) copy-start(bf16[2048,64]{0,1:T(8,128)(2,1)} %param.17) | copy-start | bytes 786436
  86.6 27.1 %copy-start.1 = (bf16[2048]{0:T(1024)(128)(2,1)S(1)}, bf16[2048]{0:T(1024)(128)(2,1)}, u32[]{:S(2)}) copy-start(bf16[2048]{0:T(1024)(128)(2,1)} %param.19) | copy-start | bytes 12292
  220.2 180.3 %copy-start.2 = (bf16[2048]{0:T(1024)(128)(2,1)S(1)}, bf16[2048]{0:T(1024)(128)(2,1)}, u32[]{:S(2)}) copy-start(bf16[2048]{0:T(1024)(128)(2,1)} %param.18) | copy-start | bytes 12292
where the time goes:
time: 825 us; the launch traced here: 824 us
  blocking collectives  682 us (83%)
  other arithmetic  70.6 us (9%)
  matrix products  65.9 us (8%)
    pmax x2, blocking collectives, reduce_col(): merged_top = lax.pmax(maxima, 'col')  153 us
    psum x2, blocking collectives, reduce_col(): merged_total = lax.psum(totals * jnp.exp(maxima - merged_top), 'col')  153 us
    psum x2, blocking collectives, reduce_row(): merged_total = lax.psum(totals * jnp.exp(maxima - merged_top), 'row')  106 us
    pmax x2, blocking collectives, reduce_row(): merged_top = lax.pmax(maxima, 'row')  106 us
    dot_general x24, matrix products, advance(): lax.dot_general(piece_desc, right_desc, (((1,), (1,)), ((), ())), preferr...  65.9 us
    reduce_sum x20, other arithmetic, advance(): row_total = jnp.sum(jnp.exp(row_score - row_top[:, None]), axis=1)  56.8 us
    all_gather x1, blocking collectives, body(): source_rows = lax.all_gather(source_desc, 'col', axis=1, tiled=True)  47.2 us
    all_gather x1, blocking collectives, body(): lax.all_gather(target_mass_piece, 'col', axis=0, tiled=True)  39.8 us

commit v1 on v0

v1 whole, which is shorter than its diff:
```python
import functools
import math

import jax
import jax.numpy as jnp
from jax import lax
from jax.experimental import pallas as pl
from jax.experimental.pallas import tpu as pltpu
from jax.sharding import PartitionSpec as P

MESH = pl.DeviceIdType.MESH
EPSILON = 0.25
REACH = 1.0
DAMPING = 1.0 / (1.0 + EPSILON / REACH)
LOG2E = math.log2(math.e)
LN2 = math.log(2.0)
SCALE = LOG2E / EPSILON
STEP = -0.5 * DAMPING
OUT = -0.5 * DAMPING * EPSILON * LN2
LANES = 128
F32 = jnp.float32
BF16 = jnp.bfloat16


def split3(value):
    high = value.astype(BF16).astype(F32)
    rest = value - high
    middle = rest.astype(BF16).astype(F32)
    low = (rest - middle).astype(BF16).astype(F32)
    return high, middle, low


def lane_block(k):
    return pl.ds(pl.multiple_of(k * LANES, LANES), LANES)


def side_rows(first, second, count):
    index = lax.broadcasted_iota(jnp.int32, (count, LANES), 0)
    rows = jnp.zeros((count, LANES), F32)
    for position, piece in enumerate(tuple(first) + tuple(second)):
        rows = jnp.where(index == position, piece, rows)
    return rows


def half_norm(points):
    return 0.5 * jnp.sum(points * points, axis=0, keepdims=True)


def right_block(b_ref, k, points):
    channels = points.shape[0]
    block = lane_block(k)
    narrow = points.astype(BF16)
    for copy in range(3):
        b_ref[copy * channels : (copy + 1) * channels, block] = narrow
    one = jnp.ones((1, LANES), F32)
    rows = side_rows((one, one, one), split3(-SCALE * half_norm(points)), 256 - 3 * channels)
    b_ref[3 * channels : 256, block] = rows.astype(BF16)


def left_block(a_ref, k, points, weight, whole):
    channels = points.shape[0]
    rows = pl.ds(pl.multiple_of(k * LANES, LANES), LANES)
    high, middle, low = split3(SCALE * points)
    if whole:
        a_ref[rows, 0:LANES] = jnp.concatenate([high, middle], axis=0).T.astype(BF16)
    one = jnp.ones((1, LANES), F32)
    side = side_rows(split3(weight - SCALE * half_norm(points)), (one, one, one), LANES - channels)
    a_ref[rows, LANES : 2 * LANES] = jnp.concatenate([low, side], axis=0).T.astype(BF16)


WIDE = 256
CHUNK = 256


def fold(value, op):
    return op(value.reshape(value.shape[0] // 8, 8, value.shape[1]), axis=0)


def emit(out_ref, j, row):
    for t in range(WIDE // LANES):
        out_ref[j * (WIDE // LANES) + t] = row[:, t * LANES : (t + 1) * LANES]


def lse_pass(a_ref, b_ref, m0, m1, out_ref):
    count = a_ref.shape[0]
    blocks = b_ref.shape[1] // WIDE
    chunks = count // CHUNK

    def product(j, i, m_ref):
        columns = pl.ds(pl.multiple_of(j * WIDE, WIDE), WIDE)
        part = jnp.dot(
            a_ref[i * CHUNK : (i + 1) * CHUNK, :], b_ref[:, columns], preferred_element_type=F32
        )
        m_ref[i * CHUNK : (i + 1) * CHUNK, :] = part
        return fold(part, jnp.max)

    def both(j, top, m_ref, next_j, next_ref):
        top = jnp.max(top, axis=0, keepdims=True)
        total = jnp.zeros((8, WIDE), F32)
        fresh = jnp.full((8, WIDE), -jnp.inf, F32)
        for i in range(chunks):
            fresh = jnp.maximum(fresh, product(next_j, i, next_ref))
            part = m_ref[i * CHUNK : (i + 1) * CHUNK, :]
            total = total + fold(jnp.exp2(part - top), jnp.sum)
        emit(out_ref, j, top + jnp.log2(jnp.sum(total, axis=0, keepdims=True)))
        return fresh

    top = jnp.full((8, WIDE), -jnp.inf, F32)
    for i in range(chunks):
        top = jnp.maximum(top, product(0, i, m0))

    def step(t, top):
        j = 2 * t
        top = both(j, top, m0, j + 1, m1)
        return both(j + 1, top, m1, lax.rem(j + 2, blocks), m0)

    lax.fori_loop(0, blocks // 2, step, top)


def kernel_pass(a_ref, b_ref, k_ref, out_ref):
    chunks = a_ref.shape[0] // CHUNK

    def step(j, carry):
        columns = pl.ds(pl.multiple_of(j * WIDE, WIDE), WIDE)
        total = jnp.zeros((8, WIDE), F32)
        for i in range(chunks):
            rows = slice(i * CHUNK, (i + 1) * CHUNK)
            part = jnp.exp2(jnp.dot(a_ref[rows, :], b_ref[:, columns], preferred_element_type=F32))
            k_ref[rows, columns] = part
            total = total + fold(part, jnp.sum)
        emit(out_ref, j, jnp.sum(total, axis=0, keepdims=True))
        return carry

    lax.fori_loop(0, b_ref.shape[1] // WIDE, step, 0)


def weighted_pass(q_ref, k_ref, out_ref):
    count = k_ref.shape[0]
    span = 8 * 16

    def column(j, carry):
        columns = pl.ds(pl.multiple_of(j * WIDE, WIDE), WIDE)

        def rows_step(i, total):
            rows = pl.ds(pl.multiple_of(i * span, span), span)
            part = k_ref[rows, columns]
            scale = q_ref[rows, :]
            return total + fold(part * jnp.concatenate([scale] * (WIDE // LANES), axis=1), jnp.sum)

        total = lax.fori_loop(0, count // span, rows_step, jnp.zeros((8, WIDE), F32), unroll=4)
        emit(out_ref, j, jnp.sum(total, axis=0, keepdims=True))
        return carry

    lax.fori_loop(0, k_ref.shape[1] // WIDE, column, 0)


def body_kernel(
    size,
    xs_ref,
    yt_ref,
    ms_ref,
    mt_ref,
    cs_ref,
    ct_ref,
    ss_ref,
    st_ref,
    xg,
    tg,
    sg,
    x32,
    ax,
    ay,
    bx,
    by,
    bs,
    bt,
    m0,
    m1,
    ks,
    kt,
    qx,
    qy,
    lms,
    lmt,
    parts,
    gathered,
    logs,
    send_sems,
    recv_sems,
):
    row, col = lax.axis_index("row"), lax.axis_index("col")
    place = {"row": row, "col": col}

    def peer(axis, k):
        return lax.rem(place[axis] + k, size)

    barrier = pltpu.get_barrier_semaphore()

    def greet(k, carry):
        for axis in ("row", "col"):
            pl.semaphore_signal(
                barrier, inc=1, device_id={axis: peer(axis, k)}, device_id_type=MESH
            )
        return carry

    lax.fori_loop(1, size, greet, 0)

    def send_all(op, axis, source_of, target):
        me = place[axis]

        def one(k, carry):
            other = peer(axis, k)
            pltpu.make_async_remote_copy(
                src_ref=source_of(other),
                dst_ref=target.at[me],
                send_sem=send_sems.at[op],
                recv_sem=recv_sems.at[op],
                device_id={axis: other},
                device_id_type=MESH,
            ).start()
            return carry

        lax.fori_loop(1, size, one, 0)

    def wait_all(sems, op, target):
        others = target.at[pl.ds(0, size - 1)]
        pltpu.make_async_copy(others, others, sems.at[op]).wait()

    pl.semaphore_wait(barrier, 2 * (size - 1))

    GX, GT, GS = 0, 1, 2
    send_all(GX, "col", lambda other: xs_ref, xg)
    send_all(GT, "col", lambda other: yt_ref.at[:, lane_block(row)], tg)

    log_mass_x = jnp.log2(ms_ref[...].astype(F32))
    log_mass_y = jnp.log2(mt_ref[...].astype(F32))
    for k in range(size):
        lms[k] = log_mass_x[k : k + 1, :]
        lmt[k] = log_mass_y[k : k + 1, :]

    def prepare_y(k, carry):
        points = yt_ref[:, lane_block(k)].astype(F32)
        right_block(by, k, points)
        left_block(ay, k, points, lmt[k], True)
        return carry

    lax.fori_loop(0, size, prepare_y, 0)
    tg[col] = yt_ref[:, lane_block(row)]
    xg[col] = xs_ref[...]

    wait_all(recv_sems, GX, xg)
    group = xs_ref.shape[0]
    for c in range(size):
        x32[c * group : (c + 1) * group, :] = xg[c].astype(F32)

    def prepare_x(k, carry):
        points = x32[:, lane_block(k)]
        right_block(bx, k, points)
        left_block(ax, k, points, lms[k], True)
        return carry

    lax.fori_loop(0, size, prepare_x, 0)
    channels = x32.shape[0]
    send_all(GS, "row", lambda other: bx.at[0:channels, lane_block(col)], sg)
    sg[row] = bx[0:channels, lane_block(col)]

    CR, CC, ST, SS = 0, 1, 2, 3
    FIRST_AXIS = ("col", "row", "col", "row")
    SECOND_AXIS = ("col", "row", "row", "col")

    def reduce_op(it, which):
        return 3 + 8 * it + which

    def gather_op(it, which):
        return 3 + 8 * it + 4 + which

    def send_parts(it, which):
        axis = FIRST_AXIS[which]
        part, inbox = parts.at[it, which], gathered.at[it, which]
        send_all(reduce_op(it, which), axis, lambda other: part.at[other], inbox)
        me = place[axis]
        inbox[me] = part[me]

    def combine(it, which):
        inbox = gathered.at[it, which]
        wait_all(recv_sems, reduce_op(it, which), inbox)
        values = inbox[...]
        if which in (CR, CC):
            top = jnp.max(values, axis=0)
            total = top + jnp.log2(jnp.sum(jnp.exp2(values - top[None]), axis=0))
        else:
            total = jnp.log2(jnp.sum(values, axis=0))
        axis = SECOND_AXIS[which]
        box = logs.at[it, which]
        me = place[axis]
        box[me] = total
        send_all(gather_op(it, which), axis, lambda other: box.at[me], box)

    def await_logs(it, which):
        wait_all(recv_sems, gather_op(it, which), logs.at[it, which])

    def prepare_right(b_ref, inbox):
        def step(k, carry):
            right_block(b_ref, k, inbox[k].astype(F32))
            return carry

        lax.fori_loop(0, size, step, 0)

    lse_pass(ay, bx, m0, m1, parts.at[0, CR])
    send_parts(0, CR)
    lse_pass(ax, by, m0, m1, parts.at[0, CC])
    send_parts(0, CC)
    wait_all(recv_sems, GT, tg)
    prepare_right(bt, tg)
    combine(0, CR)
    kernel_pass(ay, bt, kt, parts.at[0, ST])
    send_parts(0, ST)
    combine(0, CC)
    wait_all(recv_sems, GS, sg)
    prepare_right(bs, sg)
    kernel_pass(ax, bs, ks, parts.at[0, SS])
    send_parts(0, SS)
    combine(0, ST)
    await_logs(0, CR)
    await_logs(0, CC)

    def reweight(a_ref, b_ref, mass, which):
        def step(k, carry):
            points = b_ref[0:channels, lane_block(k)].astype(F32)
            left_block(a_ref, k, points, mass[k] + STEP * logs[0, which, k], False)
            return carry

        lax.fori_loop(0, size, step, 0)

    reweight(ay, by, lmt, CC)
    reweight(ax, bx, lms, CR)

    def lane_weights(q_ref, which):
        def step(k, carry):
            weight = jnp.exp2(STEP * logs[0, which, k])
            rows = pl.ds(pl.multiple_of(k * LANES, LANES), LANES)
            q_ref[rows, :] = jnp.broadcast_to(weight, (LANES, LANES)).T
            return carry

        lax.fori_loop(0, size, step, 0)

    def finish(which, out_ref):
        await_logs(1, which)
        out_ref[...] = (0.5 * OUT) * logs[0, which] + OUT * logs[1, which]

    lse_pass(ay, bx, m0, m1, parts.at[1, CR])
    send_parts(1, CR)
    combine(0, SS)
    lse_pass(ax, by, m0, m1, parts.at[1, CC])
    send_parts(1, CC)
    await_logs(0, ST)
    lane_weights(qy, ST)
    weighted_pass(qy, kt, parts.at[1, ST])
    send_parts(1, ST)
    combine(1, CR)
    combine(1, CC)
    await_logs(0, SS)
    lane_weights(qx, SS)
    weighted_pass(qx, ks, parts.at[1, SS])
    send_parts(1, SS)
    combine(1, ST)
    finish(CR, cs_ref)
    finish(CC, ct_ref)
    combine(1, SS)
    finish(ST, st_ref)
    finish(SS, ss_ref)

    wait_all(send_sems, GX, xg)
    wait_all(send_sems, GT, tg)
    wait_all(send_sems, GS, sg)
    for it in range(2):
        for which in range(4):
            wait_all(send_sems, reduce_op(it, which), gathered.at[it, which])
            wait_all(send_sems, gather_op(it, which), logs.at[it, which])


def body(size, source_desc, target_desc, source_mass, target_mass):
    count, group = source_desc.shape
    channels = target_desc.shape[1]
    vector = (size, 1, LANES)
    outs = pl.pallas_call(
        functools.partial(body_kernel, size),
        out_shape=[jax.ShapeDtypeStruct(vector, F32)] * 4,
        in_specs=[pl.BlockSpec(memory_space=pltpu.VMEM)] * 4,
        out_specs=[pl.BlockSpec(memory_space=pltpu.VMEM)] * 4,
        scratch_shapes=[
            pltpu.VMEM((size, group, count), BF16),
            pltpu.VMEM((size, channels, LANES), BF16),
            pltpu.VMEM((size, channels, LANES), BF16),
            pltpu.VMEM((channels, count), F32),
            pltpu.VMEM((count, 256), BF16),
            pltpu.VMEM((count, 256), BF16),
            pltpu.VMEM((256, count), BF16),
            pltpu.VMEM((256, count), BF16),
            pltpu.VMEM((256, count), BF16),
            pltpu.VMEM((256, count), BF16),
            pltpu.VMEM((count, WIDE), F32),
            pltpu.VMEM((count, WIDE), F32),
            pltpu.VMEM((count, count), F32),
            pltpu.VMEM((count, count), F32),
            pltpu.VMEM((count, LANES), F32),
            pltpu.VMEM((count, LANES), F32),
            pltpu.VMEM(vector, F32),
            pltpu.VMEM(vector, F32),
            pltpu.VMEM((2, 4) + vector, F32),
            pltpu.VMEM((2, 4) + vector, F32),
            pltpu.VMEM((2, 4) + vector, F32),
            pltpu.SemaphoreType.DMA((19,)),
            pltpu.SemaphoreType.DMA((19,)),
        ],
        compiler_params=pltpu.CompilerParams(
            collective_id=0, has_side_effects=True, vmem_limit_bytes=56 * 1024 * 1024
        ),
    )(
        source_desc.T,
        target_desc.T,
        source_mass.reshape(size, LANES),
        target_mass.reshape(size, LANES),
    )
    return tuple(out.reshape(count) for out in outs)


def solution(mesh):
    return jax.shard_map(
        functools.partial(body, mesh.shape["row"]),
        mesh=mesh,
        in_specs=(P("row", "col"), P("col", None), P("row"), P("col")),
        out_specs=(P("row"), P("col"), P("row"), P("col")),
        check_vma=False,
    )
```

time: 825 us -> 82.7 us (0.10)
  the two profiles are of different devices: /device:TPU:32 before, /device:TPU:1 now
where the time goes in v1:
time: 82.7 us; the launch traced here: 82.4 us
  Pallas kernels  78.3 us (95%)
  local copies, waits for them, and re-layouts  3.39 us (4%)
    pallas_call x1, Pallas kernels, body(): pl.pallas_call(functools.partial(body_kernel, size), out_shape=[jax.Shape...  78.3 us
    unnamed x12, local copies, waits for them, and re-layouts  3.39 us

profile of v1, /device:TPU:1, one launch (start us, length us, event | category | flops | bytes accessed | tf_op | source)
XLA Modules:
  0.0 82.4 jit_solution(6654348045850041313)
XLA Ops:
  0.6 78.3 %shard_map.75 = (f32[16,1,128]{2,1,0:T(1,128)}, f32[16,1,128]{2,1,0:T(1,128)}, f32[16,1,128]{2,1,0:T(1,128)}, f32[16,1,128]{2,1,0:T(1,128)}) custom-call(bf16[4,2048]{1,0:T(4,128)(2,1)} %bitcast.9, bf16[64,2048]{1,0:T(8,128)(2,1)} %bitcast.8, bf16[16,128]{1,0:T(8,128)(2,1)} %bitcast.14, bf16[16,128]{1,0:T(8,128)(2,1)} %bitcast.15), custom_call_target="tpu_custom_call" | custom-call | tf_op jit(solution)/shard_map/pallas_call | solution.py:386
  79.0 0.0 copy-start.3
  79.0 0.7 copy-done.3
  79.7 0.0 copy-start.2
  79.7 0.6 copy.12
  80.3 0.1 copy-done.2
  80.4 0.0 copy-start.1
  80.4 0.6 copy.13
  81.0 0.1 copy-done.1
  81.1 0.0 copy-start
  81.1 0.6 copy.14
  81.7 0.1 copy-done
  81.8 0.6 copy.15
Async XLA Ops:
  79.0 0.7 copy-start.3
  79.7 0.7 copy-start.2
  80.4 0.7 copy-start.1
  81.1 0.7 copy-start

commit v2 on v1

v2 whole, which is shorter than its diff:
```python
import functools
import math

import jax
import jax.numpy as jnp
from jax import lax
from jax.experimental import pallas as pl
from jax.experimental.pallas import tpu as pltpu
from jax.sharding import PartitionSpec as P

MESH = pl.DeviceIdType.MESH
EPSILON = 0.25
REACH = 1.0
DAMPING = 1.0 / (1.0 + EPSILON / REACH)
LOG2E = math.log2(math.e)
LN2 = math.log(2.0)
SCALE = LOG2E / EPSILON
STEP = -0.5 * DAMPING
OUT = -0.5 * DAMPING * EPSILON * LN2
LANES = 128
F32 = jnp.float32
BF16 = jnp.bfloat16


def split3(value):
    high = value.astype(BF16).astype(F32)
    rest = value - high
    middle = rest.astype(BF16).astype(F32)
    low = (rest - middle).astype(BF16).astype(F32)
    return high, middle, low


def lane_block(k):
    return pl.ds(pl.multiple_of(k * LANES, LANES), LANES)


def side_rows(first, second, count):
    index = lax.broadcasted_iota(jnp.int32, (count, LANES), 0)
    rows = jnp.zeros((count, LANES), F32)
    for position, piece in enumerate(tuple(first) + tuple(second)):
        rows = jnp.where(index == position, piece, rows)
    return rows


def half_norm(points):
    return 0.5 * jnp.sum(points * points, axis=0, keepdims=True)


def right_block(b_ref, k, points):
    channels = points.shape[0]
    block = lane_block(k)
    narrow = points.astype(BF16)
    for copy in range(3):
        b_ref[copy * channels : (copy + 1) * channels, block] = narrow
    one = jnp.ones((1, LANES), F32)
    rows = side_rows((one, one, one), split3(-SCALE * half_norm(points)), 256 - 3 * channels)
    b_ref[3 * channels : 256, block] = rows.astype(BF16)


def left_block(a_ref, k, points, weight, whole):
    channels = points.shape[0]
    rows = pl.ds(pl.multiple_of(k * LANES, LANES), LANES)
    high, middle, low = split3(SCALE * points)
    if whole:
        a_ref[rows, 0:LANES] = jnp.concatenate([high, middle], axis=0).T.astype(BF16)
    one = jnp.ones((1, LANES), F32)
    side = side_rows(split3(weight - SCALE * half_norm(points)), (one, one, one), LANES - channels)
    a_ref[rows, LANES : 2 * LANES] = jnp.concatenate([low, side], axis=0).T.astype(BF16)


CHUNK = 256
LSE_WIDE = 1024
KERNEL_WIDE = 1024
SUM_WIDE = 512
SPAN = 64
SUM_UNROLL = 8
UNROLL = 8


def fold(value, op):
    return op(value.reshape(value.shape[0] // 8, 8, value.shape[1]), axis=0)


def emit(out_ref, j, row, wide):
    per = wide // LANES
    for t in range(per):
        piece = row[:, t * LANES : (t + 1) * LANES]
        if len(out_ref.shape) == 3:
            out_ref[j * per + t] = piece
        else:
            out_ref[pl.ds(j * per + t, 1), :] = piece


def lse_pass(a_ref, b_ref, out_ref):
    wide = min(LSE_WIDE, b_ref.shape[1])
    chunks = a_ref.shape[0] // CHUNK

    def column(j, carry):
        columns = pl.ds(pl.multiple_of(j * wide, wide), wide)
        right = b_ref[:, columns]
        top = jnp.full((8, wide), -1e30, F32)
        total = jnp.zeros((8, wide), F32)
        for i in range(chunks):
            left = a_ref[i * CHUNK : (i + 1) * CHUNK, :]
            part = jnp.dot(left, right, preferred_element_type=F32)
            part = part.reshape(CHUNK // 8, 8, wide)
            fresh = jnp.maximum(top, jnp.max(part, axis=0))
            total = total * jnp.exp2(top - fresh) + jnp.sum(jnp.exp2(part - fresh[None]), axis=0)
            top = fresh
        peak = jnp.max(top, axis=0, keepdims=True)
        total = jnp.sum(total * jnp.exp2(top - peak), axis=0, keepdims=True)
        emit(out_ref, j, peak + jnp.log2(total), wide)
        return carry

    lax.fori_loop(0, b_ref.shape[1] // wide, column, 0)


def kernel_pass(a_ref, b_ref, k_ref, out_ref):
    wide = min(KERNEL_WIDE, b_ref.shape[1])
    chunks = a_ref.shape[0] // CHUNK

    def step(j, carry):
        columns = pl.ds(pl.multiple_of(j * wide, wide), wide)
        right = b_ref[:, columns]
        total = jnp.zeros((8, wide), F32)
        for i in range(chunks):
            rows = slice(i * CHUNK, (i + 1) * CHUNK)
            part = jnp.exp2(jnp.dot(a_ref[rows, :], right, preferred_element_type=F32))
            k_ref[rows, columns] = part
            total = total + fold(part, jnp.sum)
        emit(out_ref, j, jnp.sum(total, axis=0, keepdims=True), wide)
        return carry

    lax.fori_loop(0, b_ref.shape[1] // wide, step, 0)


def weighted_pass(q_ref, k_ref, out_ref):
    wide = min(SUM_WIDE, k_ref.shape[1])

    def column(j, carry):
        columns = pl.ds(pl.multiple_of(j * wide, wide), wide)

        def rows_step(i, total):
            rows = pl.ds(pl.multiple_of(i * SPAN, SPAN), SPAN)
            scale = jnp.concatenate([q_ref[rows, :]] * (wide // LANES), axis=1)
            return total + fold(k_ref[rows, columns] * scale, jnp.sum)

        start = jnp.zeros((8, wide), F32)
        total = lax.fori_loop(0, k_ref.shape[0] // SPAN, rows_step, start, unroll=SUM_UNROLL)
        emit(out_ref, j, jnp.sum(total, axis=0, keepdims=True), wide)
        return carry

    lax.fori_loop(0, k_ref.shape[1] // wide, column, 0)


CR, CC, ST, SS = 0, 1, 2, 3
GX, GT, GS = 0, 1, 2
OPS = 3 + 12


def body_kernel(
    size,
    xs_hbm,
    yt_hbm,
    ms_hbm,
    mt_hbm,
    out_ref,
    xs_ref,
    yt_ref,
    ms_ref,
    mt_ref,
    xg,
    tg,
    sg,
    x32,
    ax,
    ay,
    bx,
    by,
    bs,
    bt,
    ks,
    kt,
    qx,
    qy,
    lms,
    lmt,
    cross_parts,
    cross_inbox,
    cross_logs,
    self_parts,
    self_inbox,
    self_logs,
    local_sems,
    send_sems,
    recv_sems,
):
    row, col = lax.axis_index("row"), lax.axis_index("col")
    place = {"row": row, "col": col}

    def peer(axis, k):
        return lax.rem(place[axis] + k, size)

    barrier = pltpu.get_barrier_semaphore()

    def greet(k, carry):
        for axis in ("col", "row"):
            pl.semaphore_signal(
                barrier, inc=1, device_id={axis: peer(axis, k)}, device_id_type=MESH
            )
        return carry

    lax.fori_loop(1, size, greet, 0)

    loads = [
        pltpu.make_async_copy(source, target, local_sems.at[index])
        for index, (source, target) in enumerate(
            ((yt_hbm, yt_ref), (mt_hbm, mt_ref), (ms_hbm, ms_ref), (xs_hbm, xs_ref))
        )
    ]
    for load in loads:
        load.start()

    def send_all(op, axis, source_of, target):
        me = place[axis]

        def one(k, carry):
            other = peer(axis, k)
            pltpu.make_async_remote_copy(
                src_ref=source_of(other),
                dst_ref=target.at[me],
                send_sem=send_sems.at[op],
                recv_sem=recv_sems.at[op],
                device_id={axis: other},
                device_id_type=MESH,
            ).start()
            return carry

        lax.fori_loop(1, size, one, 0)

    def wait_all(sems, op, target):
        others = target.at[pl.ds(0, size - 1)]
        pltpu.make_async_copy(others, others, sems.at[op]).wait()

    def blocks(step):
        def run(k, carry):
            step(k)
            return carry

        lax.fori_loop(0, size, run, 0, unroll=UNROLL)

    for load in loads:
        load.wait()
    log_mass_x = jnp.log2(ms_ref[...].astype(F32))
    log_mass_y = jnp.log2(mt_ref[...].astype(F32))
    for k in range(size):
        lms[k] = log_mass_x[k : k + 1, :]
        lmt[k] = log_mass_y[k : k + 1, :]

    def prepare_y(k):
        points = yt_ref[:, lane_block(k)].astype(F32)
        right_block(by, k, points)
        left_block(ay, k, points, lmt[k], True)

    blocks(prepare_y)
    tg[col] = yt_ref[:, lane_block(row)]
    xg[col] = xs_ref[...]

    pl.semaphore_wait(barrier, 2 * (size - 1))
    send_all(GX, "col", lambda other: xs_ref, xg)
    send_all(GT, "col", lambda other: yt_ref.at[:, lane_block(row)], tg)

    wait_all(recv_sems, GX, xg)
    group = xs_ref.shape[0]
    for c in range(size):
        x32[c * group : (c + 1) * group, :] = xg[c].astype(F32)

    def prepare_x(k):
        points = x32[:, lane_block(k)]
        right_block(bx, k, points)
        left_block(ax, k, points, lms[k], True)

    blocks(prepare_x)
    channels = x32.shape[0]
    send_all(GS, "row", lambda other: bx.at[0:channels, lane_block(col)], sg)
    sg[row] = bx[0:channels, lane_block(col)]

    CROSS_AXIS = ("col", "row")

    def cross_op(it, which):
        return 3 + 2 * it + which

    def send_cross(it, which):
        axis = CROSS_AXIS[which]
        part, inbox = cross_parts.at[it, which], cross_inbox.at[it, which]
        send_all(cross_op(it, which), axis, lambda other: part, inbox)
        inbox[place[axis]] = part[...]

    def combine_cross(it, which):
        inbox = cross_inbox.at[it, which]
        wait_all(recv_sems, cross_op(it, which), inbox)
        values = inbox[...]
        top = jnp.max(values, axis=0)
        total = jnp.sum(jnp.exp2(values - top[None]), axis=0)
        cross_logs[it, which] = top + jnp.log2(total)

    FIRST_AXIS = {ST: "col", SS: "row"}
    SECOND_AXIS = {ST: "row", SS: "col"}

    def reduce_op(it, which):
        return 7 + 4 * it + which - ST

    def gather_op(it, which):
        return 9 + 4 * it + which - ST

    def send_self(it, which):
        axis = FIRST_AXIS[which]
        part, inbox = self_parts.at[it, which - ST], self_inbox.at[it, which - ST]
        send_all(reduce_op(it, which), axis, lambda other: part.at[other], inbox)
        me = place[axis]
        inbox[me] = part[me]

    def combine_self(it, which):
        inbox = self_inbox.at[it, which - ST]
        wait_all(recv_sems, reduce_op(it, which), inbox)
        axis = SECOND_AXIS[which]
        box = self_logs.at[it, which - ST]
        me = place[axis]
        box[me] = jnp.log2(jnp.sum(inbox[...], axis=0))
        send_all(gather_op(it, which), axis, lambda other: box.at[me], box)

    def await_self(it, which):
        wait_all(recv_sems, gather_op(it, which), self_logs.at[it, which - ST])

    def prepare_right(b_ref, inbox):
        blocks(lambda k: right_block(b_ref, k, inbox[k].astype(F32)))

    def reweight(a_ref, b_ref, mass, which):
        def step(k):
            points = b_ref[0:channels, lane_block(k)].astype(F32)
            weight = mass[k] + STEP * cross_logs[0, which, pl.ds(k, 1), :]
            left_block(a_ref, k, points, weight, False)

        blocks(step)

    def lane_weights(q_ref, which):
        def step(k):
            weight = jnp.exp2(STEP * self_logs[0, which - ST, k])
            rows = pl.ds(pl.multiple_of(k * LANES, LANES), LANES)
            q_ref[rows, :] = jnp.broadcast_to(weight, (LANES, LANES)).T

        blocks(step)

    def finish_self(which):
        await_self(1, which)
        for k in range(size):
            out_ref[which, k : k + 1, :] = (0.5 * OUT) * self_logs[0, which - ST, k] + OUT * (
                self_logs[1, which - ST, k]
            )

    def finish_cross(which):
        out_ref[which] = (0.5 * OUT) * cross_logs[0, which] + OUT * cross_logs[1, which]

    lse_pass(ax, by, cross_parts.at[0, CC])
    send_cross(0, CC)
    wait_all(recv_sems, GT, tg)
    prepare_right(bt, tg)
    kernel_pass(ay, bt, kt, self_parts.at[0, 0])
    send_self(0, ST)
    wait_all(recv_sems, GS, sg)
    prepare_right(bs, sg)
    kernel_pass(ax, bs, ks, self_parts.at[0, 1])
    send_self(0, SS)
    lse_pass(ay, bx, cross_parts.at[0, CR])
    send_cross(0, CR)
    combine_self(0, ST)
    combine_cross(0, CC)
    combine_self(0, SS)
    reweight(ay, by, lmt, CC)
    lse_pass(ay, bx, cross_parts.at[1, CR])
    send_cross(1, CR)
    await_self(0, ST)
    lane_weights(qy, ST)
    weighted_pass(qy, kt, self_parts.at[1, 0])
    send_self(1, ST)
    await_self(0, SS)
    lane_weights(qx, SS)
    weighted_pass(qx, ks, self_parts.at[1, 1])
    send_self(1, SS)
    combine_cross(0, CR)
    reweight(ax, bx, lms, CR)
    lse_pass(ax, by, cross_parts.at[1, CC])
    send_cross(1, CC)
    combine_self(1, ST)
    combine_self(1, SS)
    combine_cross(1, CR)
    finish_cross(CR)
    combine_cross(1, CC)
    finish_cross(CC)
    finish_self(ST)
    finish_self(SS)

    wait_all(send_sems, GX, xg)
    wait_all(send_sems, GT, tg)
    wait_all(send_sems, GS, sg)
    for it in range(2):
        for which in (CR, CC):
            wait_all(send_sems, cross_op(it, which), cross_inbox.at[it, which])
        for which in (ST, SS):
            wait_all(send_sems, reduce_op(it, which), self_inbox.at[it, which - ST])
            wait_all(send_sems, gather_op(it, which), self_logs.at[it, which - ST])


def unpack_kernel(all_ref, cs_ref, ct_ref, ss_ref, st_ref):
    cs_ref[...] = all_ref[CR]
    ct_ref[...] = all_ref[CC]
    ss_ref[...] = all_ref[SS]
    st_ref[...] = all_ref[ST]


def body(size, source_desc, target_desc, source_mass, target_mass):
    count, group = source_desc.shape
    channels = target_desc.shape[1]
    vector = (size, 1, LANES)
    flat = (size, LANES)
    whole = pl.BlockSpec(memory_space=pltpu.VMEM)
    packed = pl.pallas_call(
        functools.partial(body_kernel, size),
        out_shape=jax.ShapeDtypeStruct((4,) + flat, F32),
        in_specs=[pl.BlockSpec(memory_space=pl.ANY)] * 4,
        out_specs=whole,
        scratch_shapes=[
            pltpu.VMEM((group, count), BF16),
            pltpu.VMEM((channels, count), BF16),
            pltpu.VMEM(flat, BF16),
            pltpu.VMEM(flat, BF16),
            pltpu.VMEM((size, group, count), BF16),
            pltpu.VMEM((size, channels, LANES), BF16),
            pltpu.VMEM((size, channels, LANES), BF16),
            pltpu.VMEM((channels, count), F32),
            pltpu.VMEM((count, 256), BF16),
            pltpu.VMEM((count, 256), BF16),
            pltpu.VMEM((256, count), BF16),
            pltpu.VMEM((256, count), BF16),
            pltpu.VMEM((256, count), BF16),
            pltpu.VMEM((256, count), BF16),
            pltpu.VMEM((count, count), F32),
            pltpu.VMEM((count, count), F32),
            pltpu.VMEM((count, LANES), F32),
            pltpu.VMEM((count, LANES), F32),
            pltpu.VMEM(vector, F32),
            pltpu.VMEM(vector, F32),
            pltpu.VMEM((2, 2) + flat, F32),
            pltpu.VMEM((2, 2, size) + flat, F32),
            pltpu.VMEM((2, 2) + flat, F32),
            pltpu.VMEM((2, 2) + vector, F32),
            pltpu.VMEM((2, 2) + vector, F32),
            pltpu.VMEM((2, 2) + vector, F32),
            pltpu.SemaphoreType.DMA((4,)),
            pltpu.SemaphoreType.DMA((OPS,)),
            pltpu.SemaphoreType.DMA((OPS,)),
        ],
        compiler_params=pltpu.CompilerParams(
            collective_id=0, has_side_effects=True, vmem_limit_bytes=56 * 1024 * 1024
        ),
    )(
        source_desc.T,
        target_desc.T,
        source_mass.reshape(flat),
        target_mass.reshape(flat),
    )
    outs = pl.pallas_call(
        unpack_kernel,
        out_shape=[jax.ShapeDtypeStruct(flat, F32)] * 4,
        in_specs=[whole],
        out_specs=[whole] * 4,
    )(packed)
    return tuple(out.reshape(count) for out in outs)


def solution(mesh):
    return jax.shard_map(
        functools.partial(body, mesh.shape["row"]),
        mesh=mesh,
        in_specs=(P("row", "col"), P("col", None), P("row"), P("col")),
        out_specs=(P("row"), P("col"), P("row"), P("col")),
        check_vma=False,
    )
```

time: 82.7 us -> 58.8 us (0.71)
  Pallas kernels: 78.3 us -> 58 us
  local copies, waits for them, and re-layouts: 3.39 us -> 0 us
    pallas_call x1 -> x2, Pallas kernels: 78.3 us -> 58 us  [the longest x1 56.6 us: body(): pl.pallas_call(functools.partial(body_kernel, size), out_shape=jax.ShapeD...]
    unnamed x12 -> x0, local copies, waits for them, and re-layouts: 3.39 us -> none
where the time goes in v2:
time: 58.8 us; the launch traced here: 58.6 us
  Pallas kernels  58 us (99%)
  between operations  0.64 us (1%)
    pallas_call x1, Pallas kernels, body(): pl.pallas_call(functools.partial(body_kernel, size), out_shape=jax.ShapeD...  56.6 us
    pallas_call x1, Pallas kernels, body(): pl.pallas_call(unpack_kernel, out_shape=[jax.ShapeDtypeStruct(flat, F32)]...  1.37 us

profile of v2, /device:TPU:1, one launch (start us, length us, event | category | flops | bytes accessed | tf_op | source)
XLA Modules:
  0.0 58.6 jit_solution(4244837002159237263)
XLA Ops:
  0.6 56.6 %shard_map.75.all_ref = f32[4,16,128]{2,1,0:T(8,128)} custom-call(bf16[4,2048]{1,0:T(4,128)(2,1)} %bitcast.9, bf16[64,2048]{1,0:T(8,128)(2,1)} %bitcast.8, bf16[16,128]{1,0:T(8,128)(2,1)} %bitcast.10, bf16[16,128]{1,0:T(8,128)(2,1)} %bitcast.11), custom_call_target="tpu_custom_call" | custom-call | tf_op jit(solution)/shard_map/pallas_call | solution.py:427
  57.3 1.4 %shard_map.76 = (f32[16,128]{1,0:T(8,128)}, f32[16,128]{1,0:T(8,128)}, f32[16,128]{1,0:T(8,128)}, f32[16,128]{1,0:T(8,128)}) custom-call(f32[4,16,128]{2,1,0:T(8,128)} %shard_map.75.all_ref), custom_call_target="tpu_custom_call" | custom-call | tf_op jit(solution)/shard_map/pallas_call | solution.py:472

commit v3 on v2

v3 whole, which is shorter than its diff:
```python
import functools
import math

import jax
import jax.numpy as jnp
from jax import lax
from jax.experimental import pallas as pl
from jax.experimental.pallas import tpu as pltpu
from jax.sharding import PartitionSpec as P

MESH = pl.DeviceIdType.MESH
EPSILON = 0.25
REACH = 1.0
DAMPING = 1.0 / (1.0 + EPSILON / REACH)
LOG2E = math.log2(math.e)
LN2 = math.log(2.0)
SCALE = LOG2E / EPSILON
STEP = -0.5 * DAMPING
OUT = -0.5 * DAMPING * EPSILON * LN2
LANES = 128
F32 = jnp.float32
BF16 = jnp.bfloat16


def split3(value):
    high = value.astype(BF16).astype(F32)
    rest = value - high
    middle = rest.astype(BF16).astype(F32)
    low = (rest - middle).astype(BF16).astype(F32)
    return high, middle, low


def lane_block(k):
    return pl.ds(pl.multiple_of(k * LANES, LANES), LANES)


def side_rows(first, second, count):
    index = lax.broadcasted_iota(jnp.int32, (count, LANES), 0)
    rows = jnp.zeros((count, LANES), F32)
    for position, piece in enumerate(tuple(first) + tuple(second)):
        rows = jnp.where(index == position, piece, rows)
    return rows


def half_norm(points):
    return 0.5 * jnp.sum(points * points, axis=0, keepdims=True)


def right_block(b_ref, k, points):
    channels = points.shape[0]
    block = lane_block(k)
    narrow = points.astype(BF16)
    for copy in range(3):
        b_ref[copy * channels : (copy + 1) * channels, block] = narrow
    one = jnp.ones((1, LANES), F32)
    rows = side_rows((one, one, one), split3(-SCALE * half_norm(points)), 256 - 3 * channels)
    b_ref[3 * channels : 256, block] = rows.astype(BF16)


def left_block(a_ref, k, points, weight, whole):
    channels = points.shape[0]
    rows = pl.ds(pl.multiple_of(k * LANES, LANES), LANES)
    high, middle, low = split3(SCALE * points)
    if whole:
        a_ref[rows, 0:LANES] = jnp.concatenate([high, middle], axis=0).T.astype(BF16)
    one = jnp.ones((1, LANES), F32)
    side = side_rows(split3(weight - SCALE * half_norm(points)), (one, one, one), LANES - channels)
    a_ref[rows, LANES : 2 * LANES] = jnp.concatenate([low, side], axis=0).T.astype(BF16)


CHUNK = 256
LSE_WIDE = 1024
LSE_CHUNK = 128
KERNEL_WIDE = 1024
SUM_UNROLL = 4
UNROLL = 8


def fold(value, op):
    return op(value.reshape(value.shape[0] // 8, 8, value.shape[1]), axis=0)


def emit(out_ref, j, row, wide):
    per = wide // LANES
    for t in range(per):
        piece = row[:, t * LANES : (t + 1) * LANES]
        out_ref[pl.ds(j * per + t, 1), :] = piece


def lse_pass(a_ref, b_ref, held, out_ref):
    wide = held[0].shape[1]
    chunks = a_ref.shape[0] // LSE_CHUNK

    def column(j, carry):
        columns = pl.ds(pl.multiple_of(j * wide, wide), wide)
        right = b_ref[:, columns]

        def product(i):
            left = a_ref[i * LSE_CHUNK : (i + 1) * LSE_CHUNK, :]
            part = jnp.dot(left, right, preferred_element_type=F32)
            held[i % 2][...] = part
            return fold(part, jnp.max)

        top = jnp.full((8, wide), -1e30, F32)
        total = jnp.zeros((8, wide), F32)
        peak = product(0)
        for i in range(chunks):
            fresh = jnp.maximum(top, peak)
            if i + 1 < chunks:
                peak = product(i + 1)
            part = held[i % 2][...].reshape(LSE_CHUNK // 8, 8, wide)
            total = total * jnp.exp2(top - fresh) + jnp.sum(jnp.exp2(part - fresh[None]), axis=0)
            top = fresh
        peak = jnp.max(top, axis=0, keepdims=True)
        total = jnp.sum(total * jnp.exp2(top - peak), axis=0, keepdims=True)
        emit(out_ref, j, peak + jnp.log2(total), wide)
        return carry

    lax.fori_loop(0, b_ref.shape[1] // wide, column, 0)


def kernel_pass(a_ref, b_ref, k_ref, out_ref):
    wide = min(KERNEL_WIDE, b_ref.shape[1])
    chunks = a_ref.shape[0] // CHUNK

    def step(j, carry):
        columns = pl.ds(pl.multiple_of(j * wide, wide), wide)
        right = b_ref[:, columns]
        total = jnp.zeros((8, wide), F32)
        for i in range(chunks):
            rows = slice(i * CHUNK, (i + 1) * CHUNK)
            part = jnp.exp2(jnp.dot(a_ref[rows, :], right, preferred_element_type=F32))
            k_ref[rows, columns] = part
            total = total + fold(part, jnp.sum)
        emit(out_ref, j, jnp.sum(total, axis=0, keepdims=True), wide)
        return carry

    lax.fori_loop(0, b_ref.shape[1] // wide, step, 0)


def weighted_pass(q_ref, k_ref, out_ref):
    def step(i, carry):
        rows = lane_block(i)
        total = jnp.zeros((LANES, LANES), F32)
        for t in range(k_ref.shape[1] // LANES):
            total = total + k_ref[rows, t * LANES : (t + 1) * LANES] * q_ref[t : t + 1, :]
        out_ref[pl.ds(i, 1), :] = jnp.sum(fold(total.T, jnp.sum), axis=0, keepdims=True)
        return carry

    lax.fori_loop(0, k_ref.shape[0] // LANES, step, 0, unroll=SUM_UNROLL)


CR, CC, ST, SS = 0, 1, 2, 3
GX, GT, GS = 0, 1, 2
OPS = 3 + 8 + 4


def body_kernel(
    size,
    xs_hbm,
    yt_hbm,
    ms_hbm,
    mt_hbm,
    out_ref,
    xs_ref,
    yt_ref,
    ms_ref,
    mt_ref,
    xg,
    tg,
    sg,
    x32,
    ax,
    ay,
    bx,
    by,
    bs,
    bt,
    ks,
    kt,
    m0,
    m1,
    weights,
    lms,
    lmt,
    parts,
    inboxes,
    logs,
    own_logs,
    masses,
    local_sems,
    send_sems,
    recv_sems,
):
    row, col = lax.axis_index("row"), lax.axis_index("col")
    place = {"row": row, "col": col}

    def peer(axis, k):
        return lax.rem(place[axis] + k, size)

    barrier = pltpu.get_barrier_semaphore()

    def greet(k, carry):
        for axis in ("col", "row"):
            pl.semaphore_signal(
                barrier, inc=1, device_id={axis: peer(axis, k)}, device_id_type=MESH
            )
        return carry

    lax.fori_loop(1, size, greet, 0)

    loads = [
        pltpu.make_async_copy(source, target, local_sems.at[index])
        for index, (source, target) in enumerate(
            ((yt_hbm, yt_ref), (mt_hbm, mt_ref), (ms_hbm, ms_ref), (xs_hbm, xs_ref))
        )
    ]
    for load in loads:
        load.start()

    def send_all(op, axis, source, target):
        slot = target.at[place[axis]]

        def one(i, carry):
            half = (i + 1) // 2
            other = peer(axis, size // 2 + half * (2 * lax.rem(i, 2) - 1))
            pltpu.make_async_remote_copy(
                src_ref=source,
                dst_ref=slot,
                send_sem=send_sems.at[op],
                recv_sem=recv_sems.at[op],
                device_id={axis: other},
                device_id_type=MESH,
            ).start()
            return carry

        lax.fori_loop(0, size - 1, one, 0)

    def wait_all(sems, op, target):
        others = target.at[pl.ds(0, size - 1)]
        pltpu.make_async_copy(others, others, sems.at[op]).wait()

    def blocks(step):
        def run(k, carry):
            step(k)
            return carry

        lax.fori_loop(0, size, run, 0, unroll=UNROLL)

    for load in loads:
        load.wait()
    log_mass_x = jnp.log2(ms_ref[...].astype(F32))
    log_mass_y = jnp.log2(mt_ref[...].astype(F32))
    lms[...] = log_mass_x
    lmt[...] = log_mass_y

    def prepare_y(k):
        points = yt_ref[:, lane_block(k)].astype(F32)
        right_block(by, k, points)
        left_block(ay, k, points, lmt[pl.ds(k, 1), :], True)

    blocks(prepare_y)
    tg[col] = yt_ref[:, lane_block(row)]
    xg[col] = xs_ref[...]

    pl.semaphore_wait(barrier, 2 * (size - 1))
    send_all(GX, "col", xs_ref, xg)
    send_all(GT, "col", yt_ref.at[:, lane_block(row)], tg)

    for which, axis, source in ((ST, "col", lmt), (SS, "row", lms)):
        box = masses.at[which - ST]
        box[place[axis]] = source[pl.ds(place["row" if axis == "col" else "col"], 1), :]
        send_all(13 + which - ST, axis, box.at[place[axis]], box)

    wait_all(recv_sems, GX, xg)
    group = xs_ref.shape[0]
    for c in range(size):
        x32[c * group : (c + 1) * group, :] = xg[c].astype(F32)

    def prepare_x(k):
        points = x32[:, lane_block(k)]
        right_block(bx, k, points)
        left_block(ax, k, points, lms[pl.ds(k, 1), :], True)

    blocks(prepare_x)
    channels = x32.shape[0]
    send_all(GS, "row", bx.at[0:channels, lane_block(col)], sg)
    sg[row] = bx[0:channels, lane_block(col)]

    AXIS = (("col", "row", "col", "row"), ("col", "row", "row", "col"))

    def op_of(it, which):
        return 3 + 4 * it + which

    def send_parts(it, which):
        axis = AXIS[it][which]
        part, inbox = parts.at[it, which], inboxes.at[it, which]
        send_all(op_of(it, which), axis, part, inbox)
        inbox[place[axis]] = part[...]

    def own_op(which):
        return 11 + which - ST

    def send_own(which):
        box, axis = own_logs.at[which - ST], AXIS[1][which]
        me = place[axis]
        box[me] = logs[which, pl.ds(place[AXIS[0][which]], 1), :]
        send_all(own_op(which), axis, box.at[me], box)

    def combine(it, which):
        inbox = inboxes.at[it, which]
        wait_all(recv_sems, op_of(it, which), inbox)
        values = inbox[...]
        if which in (CR, CC):
            top = jnp.max(values, axis=0)
            total = top + jnp.log2(jnp.sum(jnp.exp2(values - top[None]), axis=0))
        else:
            total = jnp.log2(jnp.sum(values, axis=0))
            if it == 1:
                total = total - (lms if which == SS else lmt)[...]
        if it == 0:
            logs[which] = total
            if which in (ST, SS):
                send_own(which)
        elif which in (CR, CC):
            out_ref[which] = (0.5 * OUT) * logs[which] + OUT * total
        else:
            box = own_logs.at[which - ST]
            wait_all(recv_sems, own_op(which), box)
            for k in range(size):
                out_ref[which, k : k + 1, :] = (0.5 * OUT) * box[k] + OUT * total[k : k + 1, :]

    def prepare_right(b_ref, inbox):
        blocks(lambda k: right_block(b_ref, k, inbox[k].astype(F32)))

    def reweight(a_ref, b_ref, mass, which):
        def step(k):
            points = b_ref[0:channels, lane_block(k)].astype(F32)
            one = pl.ds(k, 1)
            left_block(a_ref, k, points, mass[one, :] + STEP * logs[which, one, :], False)

        blocks(step)

    def row_sums(k_ref, which):
        box = masses.at[which - ST]
        wait_all(recv_sems, 13 + which - ST, box)
        for k in range(size):
            weights[k : k + 1, :] = jnp.exp2(box[k] + STEP * logs[which, k : k + 1, :])
        weighted_pass(weights, k_ref, parts.at[1, which])

    held = (m0, m1)
    lse_pass(ax, by, held, parts.at[0, CC])
    send_parts(0, CC)
    lse_pass(ay, bx, held, parts.at[0, CR])
    send_parts(0, CR)
    wait_all(recv_sems, GT, tg)
    prepare_right(bt, tg)
    kernel_pass(ay, bt, kt, parts.at[0, ST])
    send_parts(0, ST)
    wait_all(recv_sems, GS, sg)
    prepare_right(bs, sg)
    kernel_pass(ax, bs, ks, parts.at[0, SS])
    send_parts(0, SS)
    combine(0, CC)
    reweight(ay, by, lmt, CC)
    lse_pass(ay, bx, held, parts.at[1, CR])
    send_parts(1, CR)
    combine(0, SS)
    row_sums(ks, SS)
    send_parts(1, SS)
    combine(0, ST)
    row_sums(kt, ST)
    send_parts(1, ST)
    combine(0, CR)
    reweight(ax, bx, lms, CR)
    lse_pass(ax, by, held, parts.at[1, CC])
    send_parts(1, CC)
    for which in (CR, SS, ST, CC):
        combine(1, which)

    wait_all(send_sems, GX, xg)
    wait_all(send_sems, GT, tg)
    wait_all(send_sems, GS, sg)
    for which in (ST, SS):
        wait_all(send_sems, 13 + which - ST, masses.at[which - ST])
        wait_all(send_sems, own_op(which), own_logs.at[which - ST])
    for it in range(2):
        for which in range(4):
            wait_all(send_sems, op_of(it, which), inboxes.at[it, which])


def unpack_kernel(all_ref, cs_ref, ct_ref, ss_ref, st_ref):
    cs_ref[...] = all_ref[CR]
    ct_ref[...] = all_ref[CC]
    ss_ref[...] = all_ref[SS]
    st_ref[...] = all_ref[ST]


def body(size, source_desc, target_desc, source_mass, target_mass):
    count, group = source_desc.shape
    channels = target_desc.shape[1]
    flat = (size, LANES)
    whole = pl.BlockSpec(memory_space=pltpu.VMEM)
    packed = pl.pallas_call(
        functools.partial(body_kernel, size),
        out_shape=jax.ShapeDtypeStruct((4,) + flat, F32),
        in_specs=[pl.BlockSpec(memory_space=pl.ANY)] * 4,
        out_specs=whole,
        scratch_shapes=[
            pltpu.VMEM((group, count), BF16),
            pltpu.VMEM((channels, count), BF16),
            pltpu.VMEM(flat, BF16),
            pltpu.VMEM(flat, BF16),
            pltpu.VMEM((size, group, count), BF16),
            pltpu.VMEM((size, channels, LANES), BF16),
            pltpu.VMEM((size, channels, LANES), BF16),
            pltpu.VMEM((channels, count), F32),
            pltpu.VMEM((count, 256), BF16),
            pltpu.VMEM((count, 256), BF16),
            pltpu.VMEM((256, count), BF16),
            pltpu.VMEM((256, count), BF16),
            pltpu.VMEM((256, count), BF16),
            pltpu.VMEM((256, count), BF16),
            pltpu.VMEM((count, count), F32),
            pltpu.VMEM((count, count), F32),
            pltpu.VMEM((LSE_CHUNK, min(LSE_WIDE, count)), F32),
            pltpu.VMEM((LSE_CHUNK, min(LSE_WIDE, count)), F32),
            pltpu.VMEM(flat, F32),
            pltpu.VMEM(flat, F32),
            pltpu.VMEM(flat, F32),
            pltpu.VMEM((2, 4) + flat, F32),
            pltpu.VMEM((2, 4, size) + flat, F32),
            pltpu.VMEM((4,) + flat, F32),
            pltpu.VMEM((2, size, 1, LANES), F32),
            pltpu.VMEM((2, size, 1, LANES), F32),
            pltpu.SemaphoreType.DMA((4,)),
            pltpu.SemaphoreType.DMA((OPS,)),
            pltpu.SemaphoreType.DMA((OPS,)),
        ],
        compiler_params=pltpu.CompilerParams(
            collective_id=0, has_side_effects=True, vmem_limit_bytes=56 * 1024 * 1024
        ),
    )(
        source_desc.T,
        target_desc.T,
        source_mass.reshape(flat),
        target_mass.reshape(flat),
    )
    outs = pl.pallas_call(
        unpack_kernel,
        out_shape=[jax.ShapeDtypeStruct(flat, F32)] * 4,
        in_specs=[whole],
        out_specs=[whole] * 4,
    )(packed)
    return tuple(out.reshape(count) for out in outs)


def solution(mesh):
    return jax.shard_map(
        functools.partial(body, mesh.shape["row"]),
        mesh=mesh,
        in_specs=(P("row", "col"), P("col", None), P("row"), P("col")),
        out_specs=(P("row"), P("col"), P("row"), P("col")),
        check_vma=False,
    )
```

time: 58.8 us -> 56.9 us (0.968)
  Pallas kernels: 58 us -> 56.1 us
    pallas_call x1, Pallas kernels: 56.6 us -> 54.7 us  [body(): pl.pallas_call(functools.partial(body_kernel, size), out_shape=jax.ShapeD...]
where the time goes in v3:
time: 56.9 us; the launch traced here: 56.7 us
  Pallas kernels  56.1 us (99%)
  between operations  0.64 us (1%)
    pallas_call x1, Pallas kernels, body(): pl.pallas_call(functools.partial(body_kernel, size), out_shape=jax.ShapeD...  54.7 us
    pallas_call x1, Pallas kernels, body(): pl.pallas_call(unpack_kernel, out_shape=[jax.ShapeDtypeStruct(flat, F32)]...  1.37 us

profile of v3, /device:TPU:1, one launch (start us, length us, event | category | flops | bytes accessed | tf_op | source)
XLA Modules:
  0.0 56.7 jit_solution(6865622496479698657)
XLA Ops:
  0.6 54.7 %shard_map.75.all_ref = f32[4,16,128]{2,1,0:T(8,128)} custom-call(bf16[4,2048]{1,0:T(4,128)(2,1)} %bitcast.9, bf16[64,2048]{1,0:T(8,128)(2,1)} %bitcast.8, bf16[16,128]{1,0:T(8,128)(2,1)} %bitcast.10, bf16[16,128]{1,0:T(8,128)(2,1)} %bitcast.11), custom_call_target="tpu_custom_call" | custom-call | tf_op jit(solution)/shard_map/pallas_call | solution.py:404
  55.4 1.4 %shard_map.76 = (f32[16,128]{1,0:T(8,128)}, f32[16,128]{1,0:T(8,128)}, f32[16,128]{1,0:T(8,128)}, f32[16,128]{1,0:T(8,128)}) custom-call(f32[4,16,128]{2,1,0:T(8,128)} %shard_map.75.all_ref), custom_call_target="tpu_custom_call" | custom-call | tf_op jit(solution)/shard_map/pallas_call | solution.py:449

commit v4 on v3

--- a/solution.py
+++ b/solution.py
@@ -87,7 +87,7 @@
         out_ref[pl.ds(j * per + t, 1), :] = piece
 
 
-def lse_pass(a_ref, b_ref, held, out_ref):
+def lse_pass(a_ref, b_ref, held, out_ref, part_index=None):
     wide = held[0].shape[1]
     chunks = a_ref.shape[0] // LSE_CHUNK
 
@@ -116,7 +116,11 @@
         emit(out_ref, j, peak + jnp.log2(total), wide)
         return carry
 
-    lax.fori_loop(0, b_ref.shape[1] // wide, column, 0)
+    blocks = b_ref.shape[1] // wide
+    if part_index is None:
+        lax.fori_loop(0, blocks, column, 0)
+    else:
+        lax.fori_loop(part_index * blocks // 2, (part_index + 1) * blocks // 2, column, 0)
 
 
 def kernel_pass(a_ref, b_ref, k_ref, out_ref):
@@ -151,8 +155,12 @@
 
 
 CR, CC, ST, SS = 0, 1, 2, 3
-GX, GT, GS = 0, 1, 2
-OPS = 3 + 8 + 4
+GS = 0
+FIRST_OP = 1
+OWN_OP = FIRST_OP + 8
+MASS_OP = OWN_OP + 2
+HALF_OP = MASS_OP + 2
+TREE_OP = HALF_OP + 1
 
 
 def body_kernel(
@@ -218,9 +226,7 @@
     for load in loads:
         load.start()
 
-    def send_all(op, axis, source, target):
-        slot = target.at[place[axis]]
-
+    def send_all(op, axis, source, slot):
         def one(i, carry):
             half = (i + 1) // 2
             other = peer(axis, size // 2 + half * (2 * lax.rem(i, 2) - 1))
@@ -236,9 +242,57 @@
 
         lax.fori_loop(0, size - 1, one, 0)
 
+    inner = math.isqrt(size)
+    outer = size // inner
+    at_outer, at_inner = col // inner, lax.rem(col, inner)
+
+    def spot(out_index, in_index):
+        return in_index * outer + out_index
+
+    def tree_send(op, box, slot, device):
+        pltpu.make_async_remote_copy(
+            src_ref=box.at[slot],
+            dst_ref=box.at[slot],
+            send_sem=send_sems.at[op],
+            recv_sem=recv_sems.at[op],
+            device_id={"col": device},
+            device_id_type=MESH,
+        ).start()
+
+    class Tree:
+        def __init__(self, first_op, box):
+            self.first_op, self.box = first_op, box
+
+        def start(self):
+            slot = spot(at_outer, at_inner)
+            for k in sorted(range(1, outer), key=lambda k: -min(k, outer - k)):
+                other = lax.rem(at_outer + k, outer)
+                tree_send(self.first_op + k, self.box, slot, other * inner + at_inner)
+            self.spread(slot)
+
+        def spread(self, slot):
+            for k in range(1, inner):
+                other = lax.rem(at_inner + k, inner)
+                tree_send(self.first_op, self.box, slot, at_outer * inner + other)
+
+        def forward(self, k):
+            slot = spot(lax.rem(at_outer + outer - k, outer), at_inner)
+            wait_one(recv_sems, self.first_op + k, self.box.at[slot])
+            self.spread(slot)
+
+        def wait(self, sems):
+            wait_one(sems, self.first_op, self.box.at[pl.ds(0, outer * (inner - 1))])
+
+        def wait_sends(self):
+            self.wait(send_sems)
+            for k in range(1, outer):
+                wait_one(send_sems, self.first_op + k, self.box.at[0])
+
+    def wait_one(sems, op, target):
+        pltpu.make_async_copy(target, target, sems.at[op]).wait()
+
     def wait_all(sems, op, target):
-        others = target.at[pl.ds(0, size - 1)]
-        pltpu.make_async_copy(others, others, sems.at[op]).wait()
+        wait_one(sems, op, target.at[pl.ds(0, size - 1)])
 
     def blocks(step):
         def run(k, carry):
@@ -260,22 +314,30 @@
         left_block(ay, k, points, lmt[pl.ds(k, 1), :], True)
 
     blocks(prepare_y)
-    tg[col] = yt_ref[:, lane_block(row)]
-    xg[col] = xs_ref[...]
+    mine = spot(at_outer, at_inner)
+    tg[mine] = yt_ref[:, lane_block(row)]
+    xg[mine] = xs_ref[...]
+    slot_of = {ST: mine, SS: row}
+    piece_of = {ST: row, SS: col}
+    for which, source in ((ST, lmt), (SS, lms)):
+        masses[which - ST, slot_of[which]] = source[pl.ds(piece_of[which], 1), :]
 
     pl.semaphore_wait(barrier, 2 * (size - 1))
-    send_all(GX, "col", xs_ref, xg)
-    send_all(GT, "col", yt_ref.at[:, lane_block(row)], tg)
-
-    for which, axis, source in ((ST, "col", lmt), (SS, "row", lms)):
-        box = masses.at[which - ST]
-        box[place[axis]] = source[pl.ds(place["row" if axis == "col" else "col"], 1), :]
-        send_all(13 + which - ST, axis, box.at[place[axis]], box)
-
-    wait_all(recv_sems, GX, xg)
+    tree_x, tree_t = Tree(TREE_OP, xg), Tree(TREE_OP + outer, tg)
+    tree_x.start()
+    tree_t.start()
+    for k in sorted(range(1, outer), key=lambda k: min(k, outer - k)):
+        tree_x.forward(k)
+        tree_t.forward(k)
+    for which, axis in ((ST, "col"), (SS, "row")):
+        slot = masses.at[which - ST, slot_of[which]]
+        send_all(MASS_OP + which - ST, axis, slot, slot)
+
+    tree_x.wait(recv_sems)
     group = xs_ref.shape[0]
     for c in range(size):
-        x32[c * group : (c + 1) * group, :] = xg[c].astype(F32)
+        block = xg[spot(c // inner, c % inner)]
+        x32[c * group : (c + 1) * group, :] = block.astype(F32)
 
     def prepare_x(k):
         points = x32[:, lane_block(k)]
@@ -284,32 +346,51 @@
 
     blocks(prepare_x)
     channels = x32.shape[0]
-    send_all(GS, "row", bx.at[0:channels, lane_block(col)], sg)
+    send_all(GS, "row", bx.at[0:channels, lane_block(col)], sg.at[row])
     sg[row] = bx[0:channels, lane_block(col)]
 
     AXIS = (("col", "row", "col", "row"), ("col", "row", "row", "col"))
 
     def op_of(it, which):
-        return 3 + 4 * it + which
+        return FIRST_OP + 4 * it + which
 
     def send_parts(it, which):
         axis = AXIS[it][which]
         part, inbox = parts.at[it, which], inboxes.at[it, which]
-        send_all(op_of(it, which), axis, part, inbox)
-        inbox[place[axis]] = part[...]
+        me = place[axis]
+        send_all(op_of(it, which), axis, part, inbox.at[me])
+        inbox[me] = part[...]
 
     def own_op(which):
-        return 11 + which - ST
+        return OWN_OP + which - ST
 
     def send_own(which):
         box, axis = own_logs.at[which - ST], AXIS[1][which]
         me = place[axis]
-        box[me] = logs[which, pl.ds(place[AXIS[0][which]], 1), :]
-        send_all(own_op(which), axis, box.at[me], box)
+        box[me] = logs[which, pl.ds(slot_of[which], 1), :]
+        send_all(own_op(which), axis, box.at[me], box.at[me])
+
+    half = size // 2
+
+    def send_half(part_index):
+        rows = pl.ds(part_index * half, half)
+        part, slot = parts.at[1, CC, rows], inboxes.at[1, CC, row, rows]
+        send_all(op_of(1, CC) if part_index == 0 else HALF_OP, "row", part, slot)
+        if part_index == 1:
+            inboxes[1, CC, row] = parts[1, CC]
+
+    def wait_parts(sems, it, which):
+        inbox = inboxes.at[it, which]
+        if (it, which) == (1, CC):
+            some = inbox.at[pl.ds(0, size - 1), pl.ds(0, half)]
+            wait_one(sems, op_of(it, which), some)
+            wait_one(sems, HALF_OP, some)
+        else:
+            wait_all(sems, op_of(it, which), inbox)
 
     def combine(it, which):
         inbox = inboxes.at[it, which]
-        wait_all(recv_sems, op_of(it, which), inbox)
+        wait_parts(recv_sems, it, which)
         values = inbox[...]
         if which in (CR, CC):
             top = jnp.max(values, axis=0)
@@ -343,7 +424,7 @@
 
     def row_sums(k_ref, which):
         box = masses.at[which - ST]
-        wait_all(recv_sems, 13 + which - ST, box)
+        wait_all(recv_sems, MASS_OP + which - ST, box)
         for k in range(size):
             weights[k : k + 1, :] = jnp.exp2(box[k] + STEP * logs[which, k : k + 1, :])
         weighted_pass(weights, k_ref, parts.at[1, which])
@@ -351,12 +432,12 @@
     held = (m0, m1)
     lse_pass(ax, by, held, parts.at[0, CC])
     send_parts(0, CC)
-    lse_pass(ay, bx, held, parts.at[0, CR])
-    send_parts(0, CR)
-    wait_all(recv_sems, GT, tg)
+    tree_t.wait(recv_sems)
     prepare_right(bt, tg)
     kernel_pass(ay, bt, kt, parts.at[0, ST])
     send_parts(0, ST)
+    lse_pass(ay, bx, held, parts.at[0, CR])
+    send_parts(0, CR)
     wait_all(recv_sems, GS, sg)
     prepare_right(bs, sg)
     kernel_pass(ax, bs, ks, parts.at[0, SS])
@@ -373,20 +454,21 @@
     send_parts(1, ST)
     combine(0, CR)
     reweight(ax, bx, lms, CR)
-    lse_pass(ax, by, held, parts.at[1, CC])
-    send_parts(1, CC)
+    for part_index in range(2):
+        lse_pass(ax, by, held, parts.at[1, CC], part_index)
+        send_half(part_index)
     for which in (CR, SS, ST, CC):
         combine(1, which)
 
-    wait_all(send_sems, GX, xg)
-    wait_all(send_sems, GT, tg)
+    tree_x.wait_sends()
+    tree_t.wait_sends()
     wait_all(send_sems, GS, sg)
     for which in (ST, SS):
-        wait_all(send_sems, 13 + which - ST, masses.at[which - ST])
+        wait_all(send_sems, MASS_OP + which - ST, masses.at[which - ST])
         wait_all(send_sems, own_op(which), own_logs.at[which - ST])
     for it in range(2):
         for which in range(4):
-            wait_all(send_sems, op_of(it, which), inboxes.at[it, which])
+            wait_parts(send_sems, it, which)
 
 
 def unpack_kernel(all_ref, cs_ref, ct_ref, ss_ref, st_ref):
@@ -400,6 +482,8 @@
     count, group = source_desc.shape
     channels = target_desc.shape[1]
     flat = (size, LANES)
+    ops = TREE_OP + 2 * (size // math.isqrt(size))
+    wide = min(LSE_WIDE, count // 2)
     whole = pl.BlockSpec(memory_space=pltpu.VMEM)
     packed = pl.pallas_call(
         functools.partial(body_kernel, size),
@@ -423,8 +507,8 @@
             pltpu.VMEM((256, count), BF16),
             pltpu.VMEM((count, count), F32),
             pltpu.VMEM((count, count), F32),
-            pltpu.VMEM((LSE_CHUNK, min(LSE_WIDE, count)), F32),
-            pltpu.VMEM((LSE_CHUNK, min(LSE_WIDE, count)), F32),
+            pltpu.VMEM((LSE_CHUNK, wide), F32),
+            pltpu.VMEM((LSE_CHUNK, wide), F32),
             pltpu.VMEM(flat, F32),
             pltpu.VMEM(flat, F32),
             pltpu.VMEM(flat, F32),
@@ -434,8 +518,8 @@
             pltpu.VMEM((2, size, 1, LANES), F32),
             pltpu.VMEM((2, size, 1, LANES), F32),
             pltpu.SemaphoreType.DMA((4,)),
-            pltpu.SemaphoreType.DMA((OPS,)),
-            pltpu.SemaphoreType.DMA((OPS,)),
+            pltpu.SemaphoreType.DMA((ops,)),
+            pltpu.SemaphoreType.DMA((ops,)),
         ],
         compiler_params=pltpu.CompilerParams(
             collective_id=0, has_side_effects=True, vmem_limit_bytes=56 * 1024 * 1024

time: 56.9 us -> 56.2 us (0.988)
  Pallas kernels: 56.1 us -> 55.4 us
    pallas_call x1, Pallas kernels: 54.7 us -> 54 us  [body(): pl.pallas_call(functools.partial(body_kernel, size), out_shape=jax.ShapeD...]
where the time goes in v4:
time: 56.2 us; the launch traced here: 56 us
  Pallas kernels  55.4 us (99%)
  between operations  0.64 us (1%)
    pallas_call x1, Pallas kernels, body(): pl.pallas_call(functools.partial(body_kernel, size), out_shape=jax.ShapeD...  54 us
    pallas_call x1, Pallas kernels, body(): pl.pallas_call(unpack_kernel, out_shape=[jax.ShapeDtypeStruct(flat, F32)]...  1.37 us

profile of v4, /device:TPU:1, one launch (start us, length us, event | category | flops | bytes accessed | tf_op | source)
XLA Modules:
  0.0 56.0 jit_solution(10091616599242609515)
XLA Ops:
  0.6 54.0 %shard_map.75.all_ref = f32[4,16,128]{2,1,0:T(8,128)} custom-call(bf16[4,2048]{1,0:T(4,128)(2,1)} %bitcast.9, bf16[64,2048]{1,0:T(8,128)(2,1)} %bitcast.8, bf16[16,128]{1,0:T(8,128)(2,1)} %bitcast.10, bf16[16,128]{1,0:T(8,128)(2,1)} %bitcast.11), custom_call_target="tpu_custom_call" | custom-call | tf_op jit(solution)/shard_map/pallas_call | solution.py:488
  54.6 1.4 %shard_map.76 = (f32[16,128]{1,0:T(8,128)}, f32[16,128]{1,0:T(8,128)}, f32[16,128]{1,0:T(8,128)}, f32[16,128]{1,0:T(8,128)}) custom-call(f32[4,16,128]{2,1,0:T(8,128)} %shard_map.75.all_ref), custom_call_target="tpu_custom_call" | custom-call | tf_op jit(solution)/shard_map/pallas_call | solution.py:533

commit v5 on v4

--- a/solution.py
+++ b/solution.py
@@ -73,6 +73,7 @@
 LSE_CHUNK = 128
 KERNEL_WIDE = 1024
 SUM_UNROLL = 4
+SEND_UNROLL = 5
 UNROLL = 8
 
 
@@ -88,7 +89,8 @@
 
 
 def lse_pass(a_ref, b_ref, held, out_ref, part_index=None):
-    wide = held[0].shape[1]
+    count = b_ref.shape[1]
+    wide = min(LSE_WIDE, count if part_index is None else count // 2)
     chunks = a_ref.shape[0] // LSE_CHUNK
 
     def column(j, carry):
@@ -98,7 +100,7 @@
         def product(i):
             left = a_ref[i * LSE_CHUNK : (i + 1) * LSE_CHUNK, :]
             part = jnp.dot(left, right, preferred_element_type=F32)
-            held[i % 2][...] = part
+            held[i % 2][:, 0:wide] = part
             return fold(part, jnp.max)
 
         top = jnp.full((8, wide), -1e30, F32)
@@ -108,7 +110,7 @@
             fresh = jnp.maximum(top, peak)
             if i + 1 < chunks:
                 peak = product(i + 1)
-            part = held[i % 2][...].reshape(LSE_CHUNK // 8, 8, wide)
+            part = held[i % 2][:, 0:wide].reshape(LSE_CHUNK // 8, 8, wide)
             total = total * jnp.exp2(top - fresh) + jnp.sum(jnp.exp2(part - fresh[None]), axis=0)
             top = fresh
         peak = jnp.max(top, axis=0, keepdims=True)
@@ -240,7 +242,7 @@
             ).start()
             return carry
 
-        lax.fori_loop(0, size - 1, one, 0)
+        lax.fori_loop(0, size - 1, one, 0, unroll=SEND_UNROLL)
 
     inner = math.isqrt(size)
     outer = size // inner
@@ -324,11 +326,11 @@
 
     pl.semaphore_wait(barrier, 2 * (size - 1))
     tree_x, tree_t = Tree(TREE_OP, xg), Tree(TREE_OP + outer, tg)
+    by_distance = sorted(range(1, outer), key=lambda k: min(k, outer - k))
     tree_x.start()
+    for k in by_distance:
+        tree_x.forward(k)
     tree_t.start()
-    for k in sorted(range(1, outer), key=lambda k: min(k, outer - k)):
-        tree_x.forward(k)
-        tree_t.forward(k)
     for which, axis in ((ST, "col"), (SS, "row")):
         slot = masses.at[which - ST, slot_of[which]]
         send_all(MASS_OP + which - ST, axis, slot, slot)
@@ -432,12 +434,14 @@
     held = (m0, m1)
     lse_pass(ax, by, held, parts.at[0, CC])
     send_parts(0, CC)
+    for k in by_distance:
+        tree_t.forward(k)
+    lse_pass(ay, bx, held, parts.at[0, CR])
+    send_parts(0, CR)
     tree_t.wait(recv_sems)
     prepare_right(bt, tg)
     kernel_pass(ay, bt, kt, parts.at[0, ST])
     send_parts(0, ST)
-    lse_pass(ay, bx, held, parts.at[0, CR])
-    send_parts(0, CR)
     wait_all(recv_sems, GS, sg)
     prepare_right(bs, sg)
     kernel_pass(ax, bs, ks, parts.at[0, SS])
@@ -446,12 +450,12 @@
     reweight(ay, by, lmt, CC)
     lse_pass(ay, bx, held, parts.at[1, CR])
     send_parts(1, CR)
+    combine(0, ST)
+    row_sums(kt, ST)
+    send_parts(1, ST)
     combine(0, SS)
     row_sums(ks, SS)
     send_parts(1, SS)
-    combine(0, ST)
-    row_sums(kt, ST)
-    send_parts(1, ST)
     combine(0, CR)
     reweight(ax, bx, lms, CR)
     for part_index in range(2):
@@ -483,7 +487,7 @@
     channels = target_desc.shape[1]
     flat = (size, LANES)
     ops = TREE_OP + 2 * (size // math.isqrt(size))
-    wide = min(LSE_WIDE, count // 2)
+    wide = min(LSE_WIDE, count)
     whole = pl.BlockSpec(memory_space=pltpu.VMEM)
     packed = pl.pallas_call(
         functools.partial(body_kernel, size),

time: 56.2 us -> 54.6 us (0.972)
  Pallas kernels: 55.4 us -> 53.8 us
    pallas_call x1, Pallas kernels: 54 us -> 52.5 us  [body(): pl.pallas_call(functools.partial(body_kernel, size), out_shape=jax.ShapeD...]
where the time goes in v5:
time: 54.6 us; the launch traced here: 54.5 us
  Pallas kernels  53.8 us (99%)
  between operations  0.64 us (1%)
    pallas_call x1, Pallas kernels, body(): pl.pallas_call(functools.partial(body_kernel, size), out_shape=jax.ShapeD...  52.5 us
    pallas_call x1, Pallas kernels, body(): pl.pallas_call(unpack_kernel, out_shape=[jax.ShapeDtypeStruct(flat, F32)]...  1.37 us

profile of v5, /device:TPU:1, one launch (start us, length us, event | category | flops | bytes accessed | tf_op | source)
XLA Modules:
  0.0 54.5 jit_solution(2248138563333272542)
XLA Ops:
  0.6 52.5 %shard_map.75.all_ref = f32[4,16,128]{2,1,0:T(8,128)} custom-call(bf16[4,2048]{1,0:T(4,128)(2,1)} %bitcast.9, bf16[64,2048]{1,0:T(8,128)(2,1)} %bitcast.8, bf16[16,128]{1,0:T(8,128)(2,1)} %bitcast.10, bf16[16,128]{1,0:T(8,128)(2,1)} %bitcast.11), custom_call_target="tpu_custom_call" | custom-call | tf_op jit(solution)/shard_map/pallas_call | solution.py:492
  53.1 1.4 %shard_map.76 = (f32[16,128]{1,0:T(8,128)}, f32[16,128]{1,0:T(8,128)}, f32[16,128]{1,0:T(8,128)}, f32[16,128]{1,0:T(8,128)}) custom-call(f32[4,16,128]{2,1,0:T(8,128)} %shard_map.75.all_ref), custom_call_target="tpu_custom_call" | custom-call | tf_op jit(solution)/shard_map/pallas_call | solution.py:537

commit v6 on v5

--- a/solution.py
+++ b/solution.py
@@ -475,11 +475,15 @@
             wait_parts(send_sems, it, which)
 
 
-def unpack_kernel(all_ref, cs_ref, ct_ref, ss_ref, st_ref):
-    cs_ref[...] = all_ref[CR]
-    ct_ref[...] = all_ref[CC]
-    ss_ref[...] = all_ref[SS]
-    st_ref[...] = all_ref[ST]
+def unpack_kernel(all_ref, cs_ref, ct_ref, ss_ref, st_ref, sems):
+    copies = [
+        pltpu.make_async_copy(all_ref.at[which], target, sems.at[which])
+        for which, target in ((CR, cs_ref), (CC, ct_ref), (SS, ss_ref), (ST, st_ref))
+    ]
+    for copy in copies:
+        copy.start()
+    for copy in copies:
+        copy.wait()
 
 
 def body(size, source_desc, target_desc, source_mass, target_mass):
@@ -537,8 +541,10 @@
     outs = pl.pallas_call(
         unpack_kernel,
         out_shape=[jax.ShapeDtypeStruct(flat, F32)] * 4,
-        in_specs=[whole],
-        out_specs=[whole] * 4,
+        in_specs=[pl.BlockSpec(memory_space=pl.ANY)],
+        out_specs=[pl.BlockSpec(memory_space=pl.ANY)] * 4,
+        scratch_shapes=[pltpu.SemaphoreType.DMA((4,))],
+        compiler_params=pltpu.CompilerParams(vmem_limit_bytes=56 * 1024 * 1024),
     )(packed)
     return tuple(out.reshape(count) for out in outs)
 

time: 54.6 us -> 55.5 us (1.016)
  Pallas kernels: 53.8 us -> 54.6 us
    pallas_call x1, Pallas kernels: 1.37 us -> 2.13 us  [body(): pl.pallas_call(unpack_kernel, out_shape=[jax.ShapeDtypeStruct(flat, F32)]...]
where the time goes in v6:
time: 55.5 us; the launch traced here: 55.4 us
  Pallas kernels  54.6 us (98%)
  between operations  0.8 us (1%)
    pallas_call x1, Pallas kernels, body(): pl.pallas_call(functools.partial(body_kernel, size), out_shape=jax.ShapeD...  52.5 us
    pallas_call x1, Pallas kernels, body(): pl.pallas_call(unpack_kernel, out_shape=[jax.ShapeDtypeStruct(flat, F32)]...  2.13 us

profile of v6, /device:TPU:1, one launch (start us, length us, event | category | flops | bytes accessed | tf_op | source)
XLA Modules:
  0.0 55.4 jit_solution(7952031030657936779)
XLA Ops:
  0.6 52.5 %shard_map.75.all_ref = f32[4,16,128]{2,1,0:T(8,128)} custom-call(bf16[4,2048]{1,0:T(4,128)(2,1)} %bitcast.9, bf16[64,2048]{1,0:T(8,128)(2,1)} %bitcast.8, bf16[16,128]{1,0:T(8,128)(2,1)} %bitcast.10, bf16[16,128]{1,0:T(8,128)(2,1)} %bitcast.11), custom_call_target="tpu_custom_call" | custom-call | tf_op jit(solution)/shard_map/pallas_call | solution.py:496
  53.1 2.1 %shard_map.76 = (f32[16,128]{1,0:T(8,128)}, f32[16,128]{1,0:T(8,128)}, f32[16,128]{1,0:T(8,128)}, f32[16,128]{1,0:T(8,128)}) custom-call(f32[4,16,128]{2,1,0:T(8,128)} %shard_map.75.all_ref), custom_call_target="tpu_custom_call" | custom-call | tf_op jit(solution)/shard_map/pallas_call | solution.py:541
